TPU v7x, 256 devices: a whole 4x4x8 slice. The times are simulated.
256 devices in a mesh: wide: 16 (over z, core), sum: 16 (over x, y).
Axes of the slice: x: 4, y: 4, z: 8, core: 2. Of those that a mesh axis runs over, the one named last changes fastest.
Arguments:
- field_pos: float32 [3, 98304], P(None, ('wide', 'sum')), may hold values from -6 to 6
- field_vel: float32 [3, 98304], P(None, ('wide', 'sum')), may hold values from -6 to 6
- field_acc: float32 [3, 98304], P(None, ('wide', 'sum')), may hold values from -6 to 6
- field_jerk: float32 [3, 98304], P(None, ('wide', 'sum')), may hold values from -6 to 6
- masses: float32 [98304], P(('wide', 'sum')), may hold values from 2.5431316e-06 to 4.0690105e-05
- levels: int32 [98304], P(('wide', 'sum')), may hold values from 0 to 3
- active_index: int32 [256, 64], P(('wide', 'sum')), may hold values from 0 to 383, as said below
- active_count: int32 [256], P(('wide', 'sum')), may hold values from 1 to 64, as said below
Outputs:
- new_pos: float32 [3, 16384], P(None, ('wide', 'sum'))
- new_vel: float32 [3, 16384], P(None, ('wide', 'sum'))
- new_acc: float32 [3, 16384], P(None, ('wide', 'sum'))
- new_jerk: float32 [3, 16384], P(None, ('wide', 'sum'))
Inputs may be any that keep to these rules, and one draw needn't show every extreme that they name: `active_index`: in each owner's row the 64 entries are distinct local indices of that owner's field stars. `active_count`: some owner has all 64 slots live.
All inputs are finite; a program needn't handle non-finite values.
Results may differ from a plain program's by a relative error of at most 0.0003.
Values sent between devices are 32-bit elements; how exact they have to be, the bound alone decides.
A program may use at most 64 MiB of HBM per device.

v0:
```python
import jax
import jax.numpy as jnp
from jax import lax
from jax.sharding import PartitionSpec as P

SOFT2 = 0.0025
STEP0 = 0.5


def predict(field_pos, field_vel, field_acc, field_jerk, levels):
    step_size = STEP0 * jnp.exp2(-levels.astype(jnp.float32))
    pred_pos = field_pos + step_size * (
        field_vel + step_size * (field_acc / 2 + step_size * field_jerk / 6)
    )
    pred_vel = field_vel + step_size * (field_acc + step_size * field_jerk / 2)
    return (step_size, pred_pos, pred_vel)


def pair_terms(actives, fpos, fvel, fmass):
    offsets = [fpos[c][None, :] - actives[c][:, None] for c in range(3)]
    motions = [fvel[c][None, :] - actives[c + 3][:, None] for c in range(3)]
    dist2 = offsets[0] * offsets[0] + offsets[1] * offsets[1] + offsets[2] * offsets[2] + SOFT2
    inverse = lax.rsqrt(dist2)
    weight = fmass[None, :] * inverse * inverse * inverse
    along = (
        3.0 * (offsets[0] * motions[0] + offsets[1] * motions[1] + offsets[2] * motions[2]) / dist2
    )
    accel = [jnp.sum(weight * offsets[c], axis=1) for c in range(3)]
    jerks = [jnp.sum(weight * (motions[c] - along * offsets[c]), axis=1) for c in range(3)]
    return jnp.stack(accel + jerks, 0)


def correct(x_old, v_old, a_old, j_old, step, acc_new, jerk_new):
    vel_new = v_old + (a_old + acc_new) * step / 2 + (j_old - jerk_new) * step * step / 12
    pos_new = x_old + (v_old + vel_new) * step / 2 + (a_old - acc_new) * step * step / 12
    return (pos_new, vel_new)


def body(field_pos, field_vel, field_acc, field_jerk, masses, levels, active_index, active_count):
    step_size, pred_pos, pred_vel = predict(field_pos, field_vel, field_acc, field_jerk, levels)
    local_ids = active_index[0]
    actives = jnp.concatenate([pred_pos[:, local_ids], pred_vel[:, local_ids]], 0)
    width = 1024

    def one_block(block):
        return pair_terms(block, pred_pos, pred_vel, masses)

    gathered = lax.all_gather(actives, "sum", axis=1, tiled=True)
    piece = lax.all_gather(gathered, "wide", axis=1, tiled=True)
    count = piece.shape[1]
    blocks = piece.reshape(6, count // width, width).transpose(1, 0, 2)
    result = lax.map(one_block, blocks)
    partials = result.transpose(1, 0, 2).reshape(6, count)
    whole = lax.psum(partials, ("wide", "sum"))
    offset = lax.axis_index(("wide", "sum")) * local_ids.shape[0]
    own_forces = lax.dynamic_slice_in_dim(whole, offset, local_ids.shape[0], 1)
    acc_new = own_forces[:3]
    jerk_new = own_forces[3:]
    step = step_size[local_ids]
    pos_new, vel_new = correct(
        field_pos[:, local_ids],
        field_vel[:, local_ids],
        field_acc[:, local_ids],
        field_jerk[:, local_ids],
        step,
        acc_new,
        jerk_new,
    )
    live = (jnp.arange(local_ids.shape[0], dtype=jnp.int32) < active_count[0])[None, :]
    zeros = jnp.zeros_like(acc_new)
    return (
        jnp.where(live, pos_new, zeros),
        jnp.where(live, vel_new, zeros),
        jnp.where(live, acc_new, zeros),
        jnp.where(live, jerk_new, zeros),
    )


def solution(mesh):
    in_specs = (
        P(None, ("wide", "sum")),
        P(None, ("wide", "sum")),
        P(None, ("wide", "sum")),
        P(None, ("wide", "sum")),
        P(("wide", "sum")),
        P(("wide", "sum")),
        P(("wide", "sum"), None),
        P(("wide", "sum")),
    )
    out_specs = (
        P(None, ("wide", "sum")),
        P(None, ("wide", "sum")),
        P(None, ("wide", "sum")),
        P(None, ("wide", "sum")),
    )
    return jax.shard_map(body, mesh=mesh, in_specs=in_specs, out_specs=out_specs, check_vma=False)
```

profile of v0, /device:TPU:224, one launch (start us, length us, event | category | flops | bytes accessed | tf_op | source)
XLA Modules:
  0.0 404.6 jit_solution(14547275354146288033)
XLA Ops:
  7.2 0.0 all-reduce.2.cloned.1.call-start
  7.2 0.7 fusion.31
  7.9 0.7 exponential_multiply_fusion
  8.6 0.8 multiply_add_fusion
  9.3 0.1 copy.138
  9.5 0.6 gather_fusion.3
  10.1 0.1 copy.140
  10.2 0.1 copy.139
  10.3 0.6 gather_fusion.4
  10.9 0.1 copy.141
  11.0 23.9 %all-gather = f32[16,64,6]{1,2,0:T(8,128)S(1)} all-gather(f32[1,64,6]{1,2,0:T(8,128)S(1)} %maximum_bitcast_fusion), channel_id=1, replica_groups=mesh['wide'=16,'sum'=16] {'sum'}, dimensions={0}, use_global_device_ids=true | all-gather | bytes 26112 | tf_op jit(solution)/shard_map/all_gather | solution.py:48
  35.0 0.1 reshape.126
  35.0 15.3 %all_gather.7 = f32[6,16384]{1,0:T(8,128)S(1)} all-gather(f32[6,1024]{1,0:T(8,128)S(1)} %bitcast.127), channel_id=1, replica_groups=mesh['wide'=16,'sum'=16] {'wide'}, dimensions={1}, use_global_device_ids=true | all-gather | bytes 417792 | tf_op jit(solution)/shard_map/all_gather | solution.py:49
  50.4 0.2 copy.159
  50.6 62.3 %while.10 = (s32[]{:T(128)}, f32[16,6,1024]{2,1,0:T(8,128)S(1)}, f32[384]{0:T(512)S(1)}, f32[3,384]{1,0:T(4,128)S(1)}, f32[16,6,1024]{2,0,1:T(8,128)S(1)}, /*ind...) while((s32[]{:T(128)}, f32[16,6,1024]{2,1,0:T(8,128)S(1)}, ...), condition=%wide.region_7.8_spmd, body=%wide.region_0.7_spmd.sunk | while | flops 15722503 | bytes 242389 | solution.py:52
  50.7 3.7 fusion.34
  54.4 0.1 stack.22
  54.6 3.7 fusion.34
  58.3 0.1 stack.22
  58.5 3.7 fusion.34
  62.2 0.1 stack.22
  62.4 3.7 fusion.34
  66.1 0.1 stack.22
  66.3 3.7 fusion.34
  70.0 0.1 stack.22
  70.2 3.7 fusion.34
  73.9 0.1 stack.22
  74.1 3.7 fusion.34
  77.8 0.1 stack.22
  78.0 3.7 fusion.34
  81.7 0.1 stack.22
  81.9 3.7 fusion.34
  85.6 0.1 stack.22
  85.8 3.7 fusion.34
  89.5 0.1 stack.22
  89.7 3.7 fusion.34
  93.4 0.1 stack.22
  93.6 3.7 fusion.34
  97.3 0.1 stack.22
  97.5 3.7 fusion.34
  101.2 0.1 stack.22
  101.4 3.7 fusion.34
  105.1 0.1 stack.22
  105.2 3.7 fusion.34
  109.0 0.1 stack.22
  109.1 3.7 fusion.34
  112.9 0.1 stack.22
  112.9 4.7 %copy.144 = f32[6,16,1024]{0,2,1:T(8,128)} copy(f32[6,16,1024]{2,0,1:T(8,128)S(1)} %bitcast.126) | data formatting | bytes 786432 | tf_op jit(solution)/shard_map/transpose | solution.py:53
  117.7 0.8 gather_fusion.5
  118.5 0.1 copy.136
  118.7 0.1 copy.137
  118.8 0.1 copy.145
  119.0 0.1 copy.135
  119.1 0.6 gather_fusion.1
  119.7 0.6 gather_fusion.2
  120.3 0.6 gather_fusion.6
  121.6 0.6 gather_fusion
  122.2 271.1 %all-reduce.2.cloned.1.call-done = f32[6,16384]{0,1:T(8,128)} async-done(((f32[6,16384]{0,1:T(8,128)}), f32[6,16384]{0,1:T(8,128)}) %all-reduce.2.cloned.1.call-update) | async-done | bytes 393232 | tf_op jit(solution)/shard_map/psum | solution.py:54
  393.2 0.9 broadcast_select_fusion
  394.2 0.9 dynamic-slice_select_fusion
  395.1 0.7 copy.146
  395.8 0.7 copy.148
  396.4 0.7 copy.149
  397.1 0.7 copy.147
  (64 shorter events, 1.4 us)
Async XLA Ops:
  7.2 43.4 %copy-start.4 = (f32[384]{0:T(512)S(1)}, f32[384]{0:T(512)}, u32[]{:S(2)}) copy-start(f32[384]{0:T(512)} %param.14) | copy-start | bytes 4612
  7.2 386.0 %all-reduce.2.cloned.1.call-start = ((), (), s32[]{:S(2)}) async-start(), calls=%async_computation | async-start | bytes 16777216 | tf_op jit(solution)/shard_map/psum | solution.py:54
  117.7 0.8 copy-start
  117.7 1.0 copy-start.1
  117.7 1.1 copy-start.2
  117.7 1.3 copy-start.3
Sparse Core Ops, SparseCore 0:
  117.8 275.3 all-reduce.1
where the time goes:
time: 410 us; the launch traced here: 405 us
  waiting for transfers between devices  271 us (66%)
  other arithmetic  63.5 us (15%)
  blocking collectives  39.3 us (10%)
  local copies, waits for them, and re-layouts  15.2 us (4%)
  between operations  14.8 us (4%)
    psum x1, waiting for transfers between devices, body(): whole = lax.psum(partials, ('wide', 'sum'))  271 us
    reduce_sum x16, other arithmetic, pair_terms(): jnp.sum(weight * (motions[c] - along * offsets[c]), axis=1)  59.5 us
    all_gather x1, blocking collectives, body(): gathered = lax.all_gather(actives, 'sum', axis=1, tiled=True)  23.9 us
    all_gather x1, blocking collectives, body(): piece = lax.all_gather(gathered, 'wide', axis=1, tiled=True)  15.3 us
  transfers between devices with their start and end apart: 1, of which 1 were waited for; matrix products, arithmetic and copies ran while one was open for 1% of the time, Pallas kernels for 0%

commit v1 on v0

v1 whole, which is shorter than its diff:
```python
import functools

import jax
import jax.numpy as jnp
from jax import lax
from jax.experimental import pallas as pl
from jax.experimental.pallas import tpu as pltpu
from jax.sharding import PartitionSpec as P

SOFT2 = 0.0025
STEP0 = 0.5
MESH = pl.DeviceIdType.MESH
F32 = jnp.float32
BF16 = jnp.bfloat16
LANES = 128
TILE = 256
STARS = 16
SOURCES = 32
VMEM_LIMIT = 63 * 1024 * 1024


def step_of(levels):
    low = jnp.where(levels == 0, STEP0, STEP0 / 2)
    high = jnp.where(levels == 2, STEP0 / 4, STEP0 / 8)
    return jnp.where(levels < 2, low, high).astype(F32)


def predict(pos, vel, acc, jerk, step):
    pred_pos = pos + step * (vel + step * (acc / 2 + step * jerk / 6))
    pred_vel = vel + step * (acc + step * jerk / 2)
    return pred_pos, pred_vel


def pieces(value):
    first = value.astype(BF16).astype(F32)
    rest = value - first
    second = rest.astype(BF16).astype(F32)
    third = (rest - second).astype(BF16).astype(F32)
    return first, second, third


def source_rows(tile):
    weight = tile[6:7]
    none = jnp.zeros_like(weight)
    sources = jnp.concatenate([weight * tile[0:3], weight, weight * tile[3:6], none], 0)
    return jnp.concatenate(list(pieces(sources)) + [jnp.zeros_like(tile)], 0)


def kernel(
    lines, planes, pos_hbm, vel_hbm, acc_hbm, jerk_hbm, mass_hbm, level_hbm, index_hbm, result,
    pos, vel, acc, jerk, mass, level, index, stage, fields, actives, arrived, partial,
    spread, moments, slot_state, sums, high_low,
    load_sem, field_send, field_recv, active_send, active_recv, part_send, part_recv,
):
    group = 2 * planes
    stars, slots = pos.shape[1], index.shape[1]
    tiles = group * slots // TILE
    share = TILE // slots
    wide, s = lax.axis_index("wide"), lax.axis_index("sum")
    z, core = wide // 2, wide % 2
    me = core * planes + s

    def line_peer(k):
        return (z + 1 + k) % lines

    def plane_peer(k):
        return (me + 1 + k) % group

    def line_id(other):
        return (other * 2 + core, s)

    def plane_id(other):
        return (z * 2 + other // planes, other % planes)

    loads = [
        pltpu.make_async_copy(source, target, load_sem.at[i])
        for i, (source, target) in enumerate(
            zip((pos_hbm, vel_hbm, acc_hbm, jerk_hbm, mass_hbm, level_hbm, index_hbm), (pos, vel, acc, jerk, mass, level, index))
        )
    ]
    for load in loads:
        load.start()

    barrier = pltpu.get_barrier_semaphore()

    def greet_line(k, carry):
        pl.semaphore_signal(barrier, inc=1, device_id=line_id(line_peer(k)), device_id_type=MESH)
        return carry

    def greet_plane(k, carry):
        pl.semaphore_signal(barrier, inc=1, device_id=plane_id(plane_peer(k)), device_id_type=MESH)
        return carry

    lax.fori_loop(0, group - 1, greet_plane, 0)
    lax.fori_loop(0, lines - 1, greet_line, 0)
    for load in loads:
        load.wait()

    step = step_of(level[...].reshape(1, stars))
    pred_pos, pred_vel = predict(pos[...], vel[...], acc[...], jerk[...], step)
    fields[z, 0:3, :] = pred_pos
    fields[z, 3:6, :] = pred_vel
    fields[z, 6:7, :] = mass[...].reshape(1, stars)
    fields[z, 7:8, :] = jnp.zeros_like(step)

    stage[0:3, :] = pos[...]
    stage[3:6, :] = vel[...]
    stage[6:9, :] = acc[...]
    stage[9:12, :] = jerk[...]
    stage[12:13, :] = step
    stage[13:16, :] = jnp.zeros((3, stars), F32)
    chosen = lax.broadcasted_iota(jnp.int32, (stars, slots), 0) == index[...]
    chosen = chosen.astype(F32).astype(BF16)
    picked = [jnp.dot(part.astype(BF16), chosen, preferred_element_type=F32) for part in pieces(stage[...])]
    picked = (picked[0] + picked[1]) + picked[2]
    result[8:24, :] = picked
    slot_pos, slot_vel = predict(picked[0:3], picked[3:6], picked[6:9], picked[9:12], picked[12:13])
    actives[me] = jnp.zeros((8, LANES), F32)
    actives[me, 0:3, 0:slots] = slot_pos
    actives[me, 3:6, 0:slots] = slot_vel

    pl.semaphore_wait(barrier, lines - 1 + group - 1)

    def line_copy(block, other, k):
        return pltpu.make_async_remote_copy(
            src_ref=fields.at[block], dst_ref=fields.at[block],
            send_sem=field_send.at[k], recv_sem=field_recv.at[block],
            device_id=line_id(other), device_id_type=MESH,
        )

    def plane_copy(block, other, k):
        return pltpu.make_async_remote_copy(
            src_ref=actives.at[block], dst_ref=actives.at[block],
            send_sem=active_send.at[k], recv_sem=active_recv.at[block],
            device_id=plane_id(other), device_id_type=MESH,
        )

    def part_copy(pair, slot, other):
        return pltpu.make_async_remote_copy(
            src_ref=partial.at[pair], dst_ref=arrived.at[slot],
            send_sem=part_send.at[other], recv_sem=part_recv.at[slot],
            device_id=plane_id(other), device_id_type=MESH,
        )

    def send_line(k, carry):
        line_copy(z, line_peer(k), k).start()
        return carry

    def send_plane(k, carry):
        plane_copy(me, plane_peer(k), k).start()
        return carry

    lax.fori_loop(0, group - 1, send_plane, 0)
    lax.fori_loop(0, lines - 1, send_line, 0)

    def take_stars(k, block):
        tile = fields[block]
        turned = jnp.concatenate([tile] + [jnp.zeros_like(tile)] * 15, 0).T
        for c in range(6):
            spread[c, k * stars:(k + 1) * stars, :] = jnp.broadcast_to(turned[:, c:c + 1], (stars, LANES))
        moments[:, k * stars:(k + 1) * stars] = source_rows(tile).astype(BF16)

    take_stars(0, z)

    def get_plane(k, carry):
        plane_copy(plane_peer(k), plane_peer(k), k).wait_recv()
        return carry

    lax.fori_loop(0, group - 1, get_plane, 0)

    lane = lax.broadcasted_iota(jnp.int32, (8, LANES), 1)

    def take_slots(i, carry):
        for pair in range(share // 2):
            o = i * share + 2 * pair
            at = pl.ds(pl.multiple_of(i * TILE + pair * LANES, LANES), LANES)
            slot_state[:, at] = jnp.where(lane < slots, actives[o], pltpu.roll(actives[o + 1], slots, 1))
        return carry

    lax.fori_loop(0, tiles, take_slots, 0)

    row = lax.broadcasted_iota(jnp.int32, (8, TILE), 0)
    blocks = 2 * stars // TILE
    rounds = lines // 2

    def weigh(at, state, buffer):
        for sub in range(0, TILE, STARS):
            star = [spread[c, at + sub:at + sub + STARS, :] for c in range(6)]
            star = [jnp.concatenate([value] * (TILE // LANES), 1) for value in star]
            r = [star[c] - state[c] for c in range(3)]
            u = [star[c + 3] - state[c + 3] for c in range(3)]
            q = r[0] * r[0] + r[1] * r[1] + (r[2] * r[2] + SOFT2)
            ru = r[0] * u[0] + r[1] * u[1] + r[2] * u[2]
            inverse = lax.rsqrt(q)
            inverse2 = inverse * inverse
            w = inverse2 * inverse
            sw = (w * inverse2) * ru
            for kind, value in enumerate((w, sw)):
                high = value.astype(BF16)
                high_low[buffer, 2 * kind, sub:sub + STARS, :] = high
                high_low[buffer, 2 * kind + 1, sub:sub + STARS, :] = (value - high.astype(F32)).astype(BF16)

    def gain(at, buffer):
        source = moments[:, at:at + TILE]
        parts = [jnp.dot(source, high_low[buffer, p], preferred_element_type=F32) for p in range(4)]
        return parts[0] + parts[1], parts[2] + parts[3]

    def finish(i):
        by_w, by_s = sums[i, 0], sums[i, 1]
        by_w = by_w[0:8] + by_w[8:16] + by_w[16:24]
        by_s = by_s[0:8] + by_s[8:16] + by_s[16:24]
        terms = by_w + pltpu.roll(jnp.where(row < 4, -3.0 * by_s, 0.0), 4, 0)
        for pair in range(share // 2):
            place = i * (share // 2) + pair
            partial[place] = terms[:, pair * LANES:(pair + 1) * LANES]
            for half in range(2):
                owner = 2 * place + half

                @pl.when(owner != me)
                def _():
                    part_copy(place, me, owner).start()

    def tile_of(j):
        return (me // share + 1 + j) % tiles

    sums[...] = jnp.zeros_like(sums)
    high_low[...] = jnp.zeros_like(high_low)
    for n in range(rounds):
        for k in (2 * n, 2 * n + 1):
            if k:
                block = (z + k) % lines
                line_copy(block, block, 0).wait_recv()
                take_stars(k, block)
        start = n * 2 * stars
        last = start + (blocks - 1) * TILE

        def add(i, terms):
            sums[i, 0] += terms[0]
            sums[i, 1] += terms[1]

        def slot_tile(j, carry, n=n, start=start, last=last, add=add):
            i = tile_of(j)
            before = jnp.where(j > 0, tile_of(j + tiles - 1), tiles)
            cols = pl.ds(pl.multiple_of(i * TILE, TILE), TILE)
            state = [jnp.broadcast_to(slot_state[c:c + 1, cols], (STARS, TILE)) for c in range(6)]
            for b in range(blocks):
                weigh(start + b * TILE, state, b)
                if b == 0:
                    add(before, gain(last, blocks - 1))
                else:
                    add(i, gain(start + (b - 1) * TILE, b - 1))
            if n == rounds - 1:

                @pl.when(j > 0)
                def _():
                    finish(before)

            return carry

        lax.fori_loop(0, tiles, slot_tile, 0)
        add(tile_of(tiles - 1), gain(last, blocks - 1))
        if n == rounds - 1:
            finish(tile_of(tiles - 1))

    arrived[me] = partial[me // 2]

    def end_line(k, carry):
        line_copy(z, line_peer(k), k).wait_send()
        return carry

    def end_plane(k, carry):
        other = plane_peer(k)
        plane_copy(me, other, k).wait_send()
        part_copy(other // 2, me, other).wait_send()
        part_copy(other // 2, other, other).wait_recv()
        return carry

    lax.fori_loop(0, lines - 1, end_line, 0)
    lax.fori_loop(0, group - 1, end_plane, 0)
    terms = jnp.sum(arrived[...], axis=0)
    terms = jnp.where(me % 2 == 0, terms, pltpu.roll(terms, slots, 1))
    result[0:8, :] = terms[:, 0:slots]


def correct_kernel(result, count, pos_hbm, vel_hbm, acc_hbm, jerk_hbm, pos, vel, acc, jerk, store_sem):
    terms, picked = result[0:8, :], result[8:24, :]
    x0, v0, a0, j0, h = picked[0:3], picked[3:6], picked[6:9], picked[9:12], picked[12:13]
    slot_pos, slot_vel = predict(x0, v0, a0, j0, h)
    new_acc = terms[0:3] - slot_pos * terms[3:4]
    new_jerk = terms[4:7] - slot_vel * terms[3:4] - slot_pos * terms[7:8]
    new_vel = v0 + (a0 + new_acc) * h / 2 + (j0 - new_jerk) * h * h / 12
    new_pos = x0 + (v0 + new_vel) * h / 2 + (a0 - new_acc) * h * h / 12
    live = lax.broadcasted_iota(jnp.int32, new_acc.shape, 1) < count[0]
    stores = []
    for i, (value, held, target) in enumerate(
        ((new_acc, acc, acc_hbm), (new_jerk, jerk, jerk_hbm), (new_vel, vel, vel_hbm), (new_pos, pos, pos_hbm))
    ):
        held[...] = jnp.where(live, value, 0.0)
        stores.append(pltpu.make_async_copy(held, target, store_sem.at[i]))
        stores[-1].start()
    for store in stores:
        store.wait()


def body(lines, planes, pos, vel, acc, jerk, masses, levels, index, count):
    stars, slots, group = pos.shape[1], index.shape[1], 2 * planes
    hbm = pl.BlockSpec(memory_space=pl.ANY)
    tiles = group * slots // TILE
    result = pl.pallas_call(
        functools.partial(kernel, lines, planes),
        out_shape=jax.ShapeDtypeStruct((24, slots), F32),
        in_specs=[hbm] * 7,
        out_specs=pl.BlockSpec(memory_space=pltpu.VMEM),
        scratch_shapes=[
            pltpu.VMEM((3, stars), F32),
            pltpu.VMEM((3, stars), F32),
            pltpu.VMEM((3, stars), F32),
            pltpu.VMEM((3, stars), F32),
            pltpu.VMEM((stars,), F32),
            pltpu.VMEM((stars,), jnp.int32),
            pltpu.VMEM((1, slots), jnp.int32),
            pltpu.VMEM((16, stars), F32),
            pltpu.VMEM((lines, 8, stars), F32),
            pltpu.VMEM((group, 8, LANES), F32),
            pltpu.VMEM((group, 8, LANES), F32),
            pltpu.VMEM((group // 2, 8, LANES), F32),
            pltpu.VMEM((6, lines * stars, LANES), F32),
            pltpu.VMEM((SOURCES, lines * stars), BF16),
            pltpu.VMEM((8, group * slots), F32),
            pltpu.VMEM((tiles + 1, 2, SOURCES, TILE), F32),
            pltpu.VMEM((2 * stars // TILE, 4, TILE, TILE), BF16),
            pltpu.SemaphoreType.DMA((7,)),
            pltpu.SemaphoreType.DMA((lines,)),
            pltpu.SemaphoreType.DMA((lines,)),
            pltpu.SemaphoreType.DMA((group,)),
            pltpu.SemaphoreType.DMA((group,)),
            pltpu.SemaphoreType.DMA((group,)),
            pltpu.SemaphoreType.DMA((group,)),
        ],
        compiler_params=pltpu.CompilerParams(collective_id=0, has_side_effects=True, vmem_limit_bytes=VMEM_LIMIT),
        name="forces",
    )(pos, vel, acc, jerk, masses, levels, index)
    three = jax.ShapeDtypeStruct((3, slots), F32)
    return pl.pallas_call(
        correct_kernel,
        out_shape=(three,) * 4,
        in_specs=[pl.BlockSpec(memory_space=pltpu.VMEM), pl.BlockSpec(memory_space=pltpu.SMEM)],
        out_specs=(hbm,) * 4,
        scratch_shapes=[pltpu.VMEM((3, slots), F32)] * 4 + [pltpu.SemaphoreType.DMA((4,))],
        compiler_params=pltpu.CompilerParams(vmem_limit_bytes=VMEM_LIMIT),
        name="correct",
    )(result, count)


def solution(mesh):
    lines, planes = mesh.shape["wide"] // 2, mesh.shape["sum"]
    both = ("wide", "sum")
    in_specs = (P(None, both),) * 4 + (P(both), P(both), P(both, None), P(both))
    return jax.shard_map(
        functools.partial(body, lines, planes), mesh=mesh, in_specs=in_specs,
        out_specs=(P(None, both),) * 4, check_vma=False,
    )
```

time: 410 us -> 60.9 us (0.15)
  the two profiles are of different devices: /device:TPU:224 before, /device:TPU:1 now
where the time goes in v1:
time: 60.9 us; the launch traced here: 60.7 us
  Pallas kernels  59.4 us (98%)
  between operations  1.29 us (2%)
    pallas_call x1, Pallas kernels, body(): pl.pallas_call(functools.partial(kernel, lines, planes), out_shape=jax.Sh...  58.1 us
    pallas_call x1, Pallas kernels, body(): pl.pallas_call(correct_kernel, out_shape=(three,) * 4, in_specs=[pl.Block...  1.33 us

profile of v1, /device:TPU:1, one launch (start us, length us, event | category | flops | bytes accessed | tf_op | source)
XLA Modules:
  0.0 60.7 jit_solution(8578274146351878969)
XLA Ops:
  1.3 58.1 %forces.1.result = f32[24,64]{1,0:T(8,128)} custom-call(f32[3,384]{1,0:T(4,128)} %pos_hbm.1, f32[3,384]{1,0:T(4,128)} %vel_hbm.1, f32[3,384]{1,0:T(4,128)} %acc_hbm.1, f32[3,384]{1,0:T(4,128)} %jerk_hbm.1, f32[384]{0:T(512)} %mass_hbm.1, s32[384]{0:T(512)} %level_hbm.1, s32[1,64]{1,0:T(1,128)} %index_hbm.1), custom_call_target="tpu_custom_call" | custom-call | tf_op jit(solution)/shard_map/forces/pallas_call | solution.py:309
  59.4 1.3 %correct.1 = (f32[3,64]{1,0:T(4,128)}, f32[3,64]{1,0:T(4,128)}, f32[3,64]{1,0:T(4,128)}, f32[3,64]{1,0:T(4,128)}) custom-call(f32[24,64]{1,0:T(8,128)} %forces.1.result, s32[1]{0:T(128)S(6)} %copy.12.count), custom_call_target="tpu_custom_call" | custom-call | tf_op jit(solution)/shard_map/correct/pallas_call | solution.py:344

commit v2 on v1

--- a/solution.py
+++ b/solution.py
@@ -14,8 +14,8 @@
 BF16 = jnp.bfloat16
 LANES = 128
 TILE = 256
-STARS = 16
-SOURCES = 32
+KDIM = 128
+ROWS = 16
 VMEM_LIMIT = 63 * 1024 * 1024
 
 
@@ -39,18 +39,57 @@
     return first, second, third
 
 
+def split_state(tile):
+    row = lax.broadcasted_iota(jnp.int32, tile.shape, 0)
+    state = jnp.where(row < 6, tile, 0.0)
+    grid = jnp.floor(state * 16.0 + 0.5) * 0.0625
+    rest = state - grid
+    near = rest.astype(BF16).astype(F32)
+    far = (rest - near).astype(BF16).astype(F32)
+    return grid, near, far
+
+
+def own_cross(grid, near, far):
+    small = near + far
+    gp, gv, sp, sv = grid[0:3], grid[3:6], small[0:3], small[3:6]
+    cross = jnp.sum(gp * gv, axis=0, keepdims=True)
+    rest = jnp.sum(gp * sv + sp * gv + sp * sv, axis=0, keepdims=True)
+    return list(pieces(cross)[:2] + pieces(rest))
+
+
+def slot_rows(tile):
+    width = tile.shape[1]
+    grid, near, far = split_state(tile)
+    none = jnp.zeros((3, width), F32)
+    own = jnp.concatenate(own_cross(grid, near, far) + [none], 0)
+    other = jnp.concatenate([jnp.ones((5, width), F32), none], 0)
+    pad = jnp.zeros((KDIM - 88, width), F32)
+    return jnp.concatenate([grid] * 3 + [near] * 3 + [far] * 3 + [own, other, pad], 0)
+
+
+def star_rows(tile):
+    width = tile.shape[1]
+    grid, near, far = split_state(tile)
+    none = jnp.zeros((3, width), F32)
+    crossed = [jnp.concatenate([-part[3:6], -part[0:3], part[6:8]], 0) for part in (grid, near, far)]
+    other = jnp.concatenate([jnp.ones((5, width), F32), none], 0)
+    own = jnp.concatenate(own_cross(grid, near, far) + [none], 0)
+    pad = jnp.zeros((KDIM - 88, width), F32)
+    return jnp.concatenate(crossed * 3 + [other, own, pad], 0)
+
+
 def source_rows(tile):
     weight = tile[6:7]
     none = jnp.zeros_like(weight)
     sources = jnp.concatenate([weight * tile[0:3], weight, weight * tile[3:6], none], 0)
-    return jnp.concatenate(list(pieces(sources)) + [jnp.zeros_like(tile)], 0)
+    return jnp.concatenate(list(pieces(sources)) + [jnp.zeros((LANES - 24, tile.shape[1]), F32)], 0)
 
 
 def kernel(
     lines, planes, pos_hbm, vel_hbm, acc_hbm, jerk_hbm, mass_hbm, level_hbm, index_hbm, result,
     pos, vel, acc, jerk, mass, level, index, stage, fields, actives, arrived, partial,
-    spread, moments, slot_state, sums, high_low,
-    load_sem, field_send, field_recv, active_send, active_recv, part_send, part_recv,
+    spread, left, place_rows, along, moments, cross, high_low, sums,
+    load_sem, ready, field_send, field_recv, active_send, active_recv, part_send, part_recv,
 ):
     group = 2 * planes
     stars, slots = pos.shape[1], index.shape[1]
@@ -61,7 +100,11 @@
     me = core * planes + s
 
     def line_peer(k):
-        return (z + 1 + k) % lines
+        other, bit = z, 1
+        while bit < lines:
+            other = other + (k // bit) % 2 * bit * (1 - 2 * ((z // bit) % 2))
+            bit *= 2
+        return other
 
     def plane_peer(k):
         return (me + 1 + k) % group
@@ -83,8 +126,8 @@
 
     barrier = pltpu.get_barrier_semaphore()
 
-    def greet_line(k, carry):
-        pl.semaphore_signal(barrier, inc=1, device_id=line_id(line_peer(k)), device_id_type=MESH)
+    def greet_line(other, carry):
+        pl.semaphore_signal(barrier, inc=1, device_id=line_id(other), device_id_type=MESH)
         return carry
 
     def greet_plane(k, carry):
@@ -92,7 +135,7 @@
         return carry
 
     lax.fori_loop(0, group - 1, greet_plane, 0)
-    lax.fori_loop(0, lines - 1, greet_line, 0)
+    lax.fori_loop(z + 1, lines, greet_line, 0)
     for load in loads:
         load.wait()
 
@@ -119,12 +162,12 @@
     actives[me, 0:3, 0:slots] = slot_pos
     actives[me, 3:6, 0:slots] = slot_vel
 
-    pl.semaphore_wait(barrier, lines - 1 + group - 1)
-
-    def line_copy(block, other, k):
+    pl.semaphore_wait(barrier, group - 1 + z)
+
+    def line_copy(block, other):
         return pltpu.make_async_remote_copy(
             src_ref=fields.at[block], dst_ref=fields.at[block],
-            send_sem=field_send.at[k], recv_sem=field_recv.at[block],
+            send_sem=field_send.at[other], recv_sem=field_recv.at[block],
             device_id=line_id(other), device_id_type=MESH,
         )
 
@@ -142,8 +185,14 @@
             device_id=plane_id(other), device_id_type=MESH,
         )
 
-    def send_line(k, carry):
-        line_copy(z, line_peer(k), k).start()
+    def send_lower(other, carry):
+        pl.semaphore_signal(ready.at[z], inc=1, device_id=line_id(other), device_id_type=MESH)
+        line_copy(z, other).start()
+        return carry
+
+    def send_higher(other, carry):
+        pl.semaphore_wait(ready.at[other], 1)
+        line_copy(z, other).start()
         return carry
 
     def send_plane(k, carry):
@@ -151,14 +200,19 @@
         return carry
 
     lax.fori_loop(0, group - 1, send_plane, 0)
-    lax.fori_loop(0, lines - 1, send_line, 0)
+    lax.fori_loop(0, z, send_lower, 0)
 
     def take_stars(k, block):
         tile = fields[block]
-        turned = jnp.concatenate([tile] + [jnp.zeros_like(tile)] * 15, 0).T
-        for c in range(6):
-            spread[c, k * stars:(k + 1) * stars, :] = jnp.broadcast_to(turned[:, c:c + 1], (stars, LANES))
-        moments[:, k * stars:(k + 1) * stars] = source_rows(tile).astype(BF16)
+        at = pl.ds(pl.multiple_of(k * stars, LANES), stars)
+        place_rows[:, at] = tile
+        along[:, at] = star_rows(tile).astype(BF16)
+        turned = source_rows(tile).T.astype(BF16)
+        for sub in range(0, stars, LANES):
+            first = k * stars + sub
+            tall = first // TILE * 2 * TILE + first % TILE
+            for part in range(2):
+                moments[pl.ds(pl.multiple_of(tall + part * TILE, LANES), LANES), :] = turned[sub:sub + LANES]
 
     take_stars(0, z)
 
@@ -170,46 +224,63 @@
 
     lane = lax.broadcasted_iota(jnp.int32, (8, LANES), 1)
 
-    def take_slots(i, carry):
-        for pair in range(share // 2):
-            o = i * share + 2 * pair
-            at = pl.ds(pl.multiple_of(i * TILE + pair * LANES, LANES), LANES)
-            slot_state[:, at] = jnp.where(lane < slots, actives[o], pltpu.roll(actives[o + 1], slots, 1))
-        return carry
-
-    lax.fori_loop(0, tiles, take_slots, 0)
-
-    row = lax.broadcasted_iota(jnp.int32, (8, TILE), 0)
+    def take_slots(pair, carry):
+        tile = jnp.where(lane < slots, actives[2 * pair], pltpu.roll(actives[2 * pair + 1], slots, 1))
+        at = pl.ds(pl.multiple_of(pair * LANES, LANES), LANES)
+        left[at, :] = slot_rows(tile).T.astype(BF16)
+        turned = jnp.concatenate([tile] + [jnp.zeros_like(tile)] * 15, 0).T
+        for c in range(3):
+            spread[c, at, :] = jnp.broadcast_to(turned[:, c:c + 1], (LANES, LANES))
+        return carry
+
+    lax.fori_loop(0, group // 2, take_slots, 0)
+
+    @pl.when(z % 2 == 0)
+    def _():
+        send_higher(z + 1, 0)
+
+    line_copy(line_peer(1), line_peer(1)).wait_recv()
+    take_stars(1, line_peer(1))
+
     blocks = 2 * stars // TILE
     rounds = lines // 2
 
-    def weigh(at, state, buffer):
-        for sub in range(0, TILE, STARS):
-            star = [spread[c, at + sub:at + sub + STARS, :] for c in range(6)]
-            star = [jnp.concatenate([value] * (TILE // LANES), 1) for value in star]
-            r = [star[c] - state[c] for c in range(3)]
-            u = [star[c + 3] - state[c + 3] for c in range(3)]
+    def stars_of(n, b):
+        return pl.ds(pl.multiple_of((n * blocks + b) * TILE, TILE), TILE)
+
+    def get_cross(n, i, b):
+        rows = pl.ds(pl.multiple_of(i * TILE, TILE), TILE)
+        cross[b] = jnp.dot(left[rows, :], along[:, stars_of(n, b)], preferred_element_type=F32)
+
+    def weigh(n, i, b, side):
+        state = [jnp.broadcast_to(place_rows[c:c + 1, stars_of(n, b)], (ROWS, TILE)) for c in range(3)]
+        high_at = slice(2 * b * TILE, (2 * b + 1) * TILE)
+        low_at = slice((2 * b + 1) * TILE, (2 * b + 2) * TILE)
+        for sub in range(0, TILE, ROWS):
+            rows = pl.ds(pl.multiple_of(i * TILE + sub, ROWS), ROWS)
+            slot = [jnp.concatenate([spread[c, rows, :]] * (TILE // LANES), 1) for c in range(3)]
+            r = [state[c] - slot[c] for c in range(3)]
             q = r[0] * r[0] + r[1] * r[1] + (r[2] * r[2] + SOFT2)
-            ru = r[0] * u[0] + r[1] * u[1] + r[2] * u[2]
             inverse = lax.rsqrt(q)
             inverse2 = inverse * inverse
             w = inverse2 * inverse
-            sw = (w * inverse2) * ru
+            sw = (w * inverse2) * cross[b, sub:sub + ROWS, :]
             for kind, value in enumerate((w, sw)):
                 high = value.astype(BF16)
-                high_low[buffer, 2 * kind, sub:sub + STARS, :] = high
-                high_low[buffer, 2 * kind + 1, sub:sub + STARS, :] = (value - high.astype(F32)).astype(BF16)
-
-    def gain(at, buffer):
-        source = moments[:, at:at + TILE]
-        parts = [jnp.dot(source, high_low[buffer, p], preferred_element_type=F32) for p in range(4)]
-        return parts[0] + parts[1], parts[2] + parts[3]
+                high_low[side, kind, sub:sub + ROWS, high_at] = high
+                high_low[side, kind, sub:sub + ROWS, low_at] = (value - high.astype(F32)).astype(BF16)
+
+    def gain(n, side, kind):
+        source = moments[pl.ds(pl.multiple_of(n * 2 * blocks * TILE, TILE), 2 * blocks * TILE), :]
+        return jnp.dot(high_low[side, kind], source, preferred_element_type=F32)
+
+    def add(i, by_w, by_s):
+        lane = lax.broadcasted_iota(jnp.int32, (TILE, LANES), 1) % 8
+        sums[i] += by_w + pltpu.roll(jnp.where(lane < 4, -3.0 * by_s, 0.0), 4, 1)
 
     def finish(i):
-        by_w, by_s = sums[i, 0], sums[i, 1]
-        by_w = by_w[0:8] + by_w[8:16] + by_w[16:24]
-        by_s = by_s[0:8] + by_s[8:16] + by_s[16:24]
-        terms = by_w + pltpu.roll(jnp.where(row < 4, -3.0 * by_s, 0.0), 4, 0)
+        turned = sums[i].T
+        terms = turned[0:8] + turned[8:16] + turned[16:24]
         for pair in range(share // 2):
             place = i * (share // 2) + pair
             partial[place] = terms[:, pair * LANES:(pair + 1) * LANES]
@@ -224,48 +295,60 @@
         return (me // share + 1 + j) % tiles
 
     sums[...] = jnp.zeros_like(sums)
-    high_low[...] = jnp.zeros_like(high_low)
-    for n in range(rounds):
-        for k in (2 * n, 2 * n + 1):
-            if k:
-                block = (z + k) % lines
-                line_copy(block, block, 0).wait_recv()
-                take_stars(k, block)
-        start = n * 2 * stars
-        last = start + (blocks - 1) * TILE
-
-        def add(i, terms):
-            sums[i, 0] += terms[0]
-            sums[i, 1] += terms[1]
-
-        def slot_tile(j, carry, n=n, start=start, last=last, add=add):
-            i = tile_of(j)
-            before = jnp.where(j > 0, tile_of(j + tiles - 1), tiles)
-            cols = pl.ds(pl.multiple_of(i * TILE, TILE), TILE)
-            state = [jnp.broadcast_to(slot_state[c:c + 1, cols], (STARS, TILE)) for c in range(6)]
-            for b in range(blocks):
-                weigh(start + b * TILE, state, b)
-                if b == 0:
-                    add(before, gain(last, blocks - 1))
-                else:
-                    add(i, gain(start + (b - 1) * TILE, b - 1))
-            if n == rounds - 1:
-
-                @pl.when(j > 0)
-                def _():
+
+    def pair_round(n, final):
+        get_cross(n, tile_of(0), 0)
+
+        def two_tiles(pair, carry):
+            for side in range(2):
+                j = 2 * pair + side
+                i, after = tile_of(j), tile_of(j + 1)
+                before = tile_of(j + tiles - 1) if side else jnp.where(j > 0, tile_of(j + tiles - 1), tiles)
+                found = []
+                for b in range(blocks):
+                    if b < blocks - 1:
+                        get_cross(n, i, b + 1)
+                    else:
+                        get_cross(n, after, 0)
+                    weigh(n, i, b, side)
+                    if b < 2:
+                        found.append(gain(n, 1 - side, b))
+                add(before, *found)
+                if final and side:
                     finish(before)
+                elif final:
+
+                    @pl.when(j > 0)
+                    def _():
+                        finish(before)
 
             return carry
 
-        lax.fori_loop(0, tiles, slot_tile, 0)
-        add(tile_of(tiles - 1), gain(last, blocks - 1))
-        if n == rounds - 1:
+        lax.fori_loop(0, tiles // 2, two_tiles, 0)
+        add(tile_of(tiles - 1), gain(n, 1, 0), gain(n, 1, 1))
+        if final:
             finish(tile_of(tiles - 1))
 
+    def early_round(n, carry):
+        pair_round(n, False)
+
+        @pl.when(n == 0)
+        def _():
+            lax.fori_loop(z + 2 - z % 2, lines, send_higher, 0)
+
+        for k in (2 * n + 2, 2 * n + 3):
+            block = line_peer(k)
+            line_copy(block, block).wait_recv()
+            take_stars(k, block)
+        return carry
+
+    lax.fori_loop(0, rounds - 1, early_round, 0)
+    pair_round(rounds - 1, True)
+
     arrived[me] = partial[me // 2]
 
     def end_line(k, carry):
-        line_copy(z, line_peer(k), k).wait_send()
+        line_copy(z, line_peer(k + 1)).wait_send()
         return carry
 
     def end_plane(k, carry):
@@ -305,7 +388,7 @@
 def body(lines, planes, pos, vel, acc, jerk, masses, levels, index, count):
     stars, slots, group = pos.shape[1], index.shape[1], 2 * planes
     hbm = pl.BlockSpec(memory_space=pl.ANY)
-    tiles = group * slots // TILE
+    tiles, blocks = group * slots // TILE, 2 * stars // TILE
     result = pl.pallas_call(
         functools.partial(kernel, lines, planes),
         out_shape=jax.ShapeDtypeStruct((24, slots), F32),
@@ -324,12 +407,16 @@
             pltpu.VMEM((group, 8, LANES), F32),
             pltpu.VMEM((group, 8, LANES), F32),
             pltpu.VMEM((group // 2, 8, LANES), F32),
-            pltpu.VMEM((6, lines * stars, LANES), F32),
-            pltpu.VMEM((SOURCES, lines * stars), BF16),
-            pltpu.VMEM((8, group * slots), F32),
-            pltpu.VMEM((tiles + 1, 2, SOURCES, TILE), F32),
-            pltpu.VMEM((2 * stars // TILE, 4, TILE, TILE), BF16),
+            pltpu.VMEM((3, group * slots, LANES), F32),
+            pltpu.VMEM((group * slots, KDIM), BF16),
+            pltpu.VMEM((8, lines * stars), F32),
+            pltpu.VMEM((KDIM, lines * stars), BF16),
+            pltpu.VMEM((2 * lines * stars, LANES), BF16),
+            pltpu.VMEM((blocks, TILE, TILE), F32),
+            pltpu.VMEM((2, 2, TILE, 2 * blocks * TILE), BF16),
+            pltpu.VMEM((tiles + 1, TILE, LANES), F32),
             pltpu.SemaphoreType.DMA((7,)),
+            pltpu.SemaphoreType.REGULAR((lines,)),
             pltpu.SemaphoreType.DMA((lines,)),
             pltpu.SemaphoreType.DMA((lines,)),
             pltpu.SemaphoreType.DMA((group,)),

time: 60.9 us -> 66.2 us (1.087)
  the two profiles are of different devices: /device:TPU:1 before, /device:TPU:224 now
where the time goes in v2:
time: 66.2 us; the launch traced here: 66 us
  Pallas kernels  64.7 us (98%)
  between operations  1.29 us (2%)
    pallas_call x1, Pallas kernels, body(): pl.pallas_call(functools.partial(kernel, lines, planes), out_shape=jax.Sh...  63.4 us
    pallas_call x1, Pallas kernels, body(): pl.pallas_call(correct_kernel, out_shape=(three,) * 4, in_specs=[pl.Block...  1.33 us

profile of v2, /device:TPU:224, one launch (start us, length us, event | category | flops | bytes accessed | tf_op | source)
XLA Modules:
  0.0 66.0 jit_solution(16536266711664790798)
XLA Ops:
  1.3 63.4 %forces.1.result = f32[24,64]{1,0:T(8,128)} custom-call(f32[3,384]{1,0:T(4,128)} %pos_hbm.1, f32[3,384]{1,0:T(4,128)} %vel_hbm.1, f32[3,384]{1,0:T(4,128)} %acc_hbm.1, f32[3,384]{1,0:T(4,128)} %jerk_hbm.1, f32[384]{0:T(512)} %mass_hbm.1, s32[384]{0:T(512)} %level_hbm.1, s32[1,64]{1,0:T(1,128)} %index_hbm.1), custom_call_target="tpu_custom_call" | custom-call | tf_op jit(solution)/shard_map/forces/pallas_call | solution.py:392
  64.7 1.3 %correct.1 = (f32[3,64]{1,0:T(4,128)}, f32[3,64]{1,0:T(4,128)}, f32[3,64]{1,0:T(4,128)}, f32[3,64]{1,0:T(4,128)}) custom-call(f32[24,64]{1,0:T(8,128)} %forces.1.result, s32[1]{0:T(128)S(6)} %copy.12.count), custom_call_target="tpu_custom_call" | custom-call | tf_op jit(solution)/shard_map/correct/pallas_call | solution.py:431

commit v3 on v2

--- a/solution.py
+++ b/solution.py
@@ -16,6 +16,7 @@
 TILE = 256
 KDIM = 128
 ROWS = 16
+SOURCES = 32
 VMEM_LIMIT = 63 * 1024 * 1024
 
 
@@ -82,7 +83,7 @@
     weight = tile[6:7]
     none = jnp.zeros_like(weight)
     sources = jnp.concatenate([weight * tile[0:3], weight, weight * tile[3:6], none], 0)
-    return jnp.concatenate(list(pieces(sources)) + [jnp.zeros((LANES - 24, tile.shape[1]), F32)], 0)
+    return jnp.concatenate(list(pieces(sources)) + [jnp.zeros((SOURCES - 24, tile.shape[1]), F32)], 0)
 
 
 def kernel(
@@ -205,14 +206,11 @@
     def take_stars(k, block):
         tile = fields[block]
         at = pl.ds(pl.multiple_of(k * stars, LANES), stars)
-        place_rows[:, at] = tile
-        along[:, at] = star_rows(tile).astype(BF16)
-        turned = source_rows(tile).T.astype(BF16)
-        for sub in range(0, stars, LANES):
-            first = k * stars + sub
-            tall = first // TILE * 2 * TILE + first % TILE
-            for part in range(2):
-                moments[pl.ds(pl.multiple_of(tall + part * TILE, LANES), LANES), :] = turned[sub:sub + LANES]
+        left[at, :] = star_rows(tile).T.astype(BF16)
+        turned = jnp.concatenate([tile] + [jnp.zeros_like(tile)] * 15, 0).T
+        for c in range(3):
+            spread[c, at, :] = jnp.broadcast_to(turned[:, c:c + 1], (stars, LANES))
+        moments[:, at] = source_rows(tile).astype(BF16)
 
     take_stars(0, z)
 
@@ -227,10 +225,8 @@
     def take_slots(pair, carry):
         tile = jnp.where(lane < slots, actives[2 * pair], pltpu.roll(actives[2 * pair + 1], slots, 1))
         at = pl.ds(pl.multiple_of(pair * LANES, LANES), LANES)
-        left[at, :] = slot_rows(tile).T.astype(BF16)
-        turned = jnp.concatenate([tile] + [jnp.zeros_like(tile)] * 15, 0).T
-        for c in range(3):
-            spread[c, at, :] = jnp.broadcast_to(turned[:, c:c + 1], (LANES, LANES))
+        place_rows[:, at] = tile
+        along[:, at] = slot_rows(tile).astype(BF16)
         return carry
 
     lax.fori_loop(0, group // 2, take_slots, 0)
@@ -248,18 +244,18 @@
     def stars_of(n, b):
         return pl.ds(pl.multiple_of((n * blocks + b) * TILE, TILE), TILE)
 
+    def slots_of(i):
+        return pl.ds(pl.multiple_of(i * TILE, TILE), TILE)
+
     def get_cross(n, i, b):
-        rows = pl.ds(pl.multiple_of(i * TILE, TILE), TILE)
-        cross[b] = jnp.dot(left[rows, :], along[:, stars_of(n, b)], preferred_element_type=F32)
-
-    def weigh(n, i, b, side):
-        state = [jnp.broadcast_to(place_rows[c:c + 1, stars_of(n, b)], (ROWS, TILE)) for c in range(3)]
-        high_at = slice(2 * b * TILE, (2 * b + 1) * TILE)
-        low_at = slice((2 * b + 1) * TILE, (2 * b + 2) * TILE)
+        cross[b] = jnp.dot(left[stars_of(n, b), :], along[:, slots_of(i)], preferred_element_type=F32)
+
+    def weigh(n, i, b):
+        state = [jnp.broadcast_to(place_rows[c:c + 1, slots_of(i)], (ROWS, TILE)) for c in range(3)]
         for sub in range(0, TILE, ROWS):
-            rows = pl.ds(pl.multiple_of(i * TILE + sub, ROWS), ROWS)
-            slot = [jnp.concatenate([spread[c, rows, :]] * (TILE // LANES), 1) for c in range(3)]
-            r = [state[c] - slot[c] for c in range(3)]
+            rows = pl.ds(pl.multiple_of((n * blocks + b) * TILE + sub, ROWS), ROWS)
+            star = [jnp.concatenate([spread[c, rows, :]] * (TILE // LANES), 1) for c in range(3)]
+            r = [star[c] - state[c] for c in range(3)]
             q = r[0] * r[0] + r[1] * r[1] + (r[2] * r[2] + SOFT2)
             inverse = lax.rsqrt(q)
             inverse2 = inverse * inverse
@@ -267,20 +263,21 @@
             sw = (w * inverse2) * cross[b, sub:sub + ROWS, :]
             for kind, value in enumerate((w, sw)):
                 high = value.astype(BF16)
-                high_low[side, kind, sub:sub + ROWS, high_at] = high
-                high_low[side, kind, sub:sub + ROWS, low_at] = (value - high.astype(F32)).astype(BF16)
-
-    def gain(n, side, kind):
-        source = moments[pl.ds(pl.multiple_of(n * 2 * blocks * TILE, TILE), 2 * blocks * TILE), :]
-        return jnp.dot(high_low[side, kind], source, preferred_element_type=F32)
-
-    def add(i, by_w, by_s):
-        lane = lax.broadcasted_iota(jnp.int32, (TILE, LANES), 1) % 8
-        sums[i] += by_w + pltpu.roll(jnp.where(lane < 4, -3.0 * by_s, 0.0), 4, 1)
+                high_low[b, kind, sub:sub + ROWS, :] = high
+                high_low[b, kind, TILE + sub:TILE + sub + ROWS, :] = (value - high.astype(F32)).astype(BF16)
+
+    def gain(n, i, b):
+        source = moments[:, stars_of(n, b)]
+        source = jnp.concatenate([source, source], 1)
+        for kind in range(2):
+            sums[i, kind] += jnp.dot(source, high_low[b, kind], preferred_element_type=F32)
 
     def finish(i):
-        turned = sums[i].T
-        terms = turned[0:8] + turned[8:16] + turned[16:24]
+        by_w, by_s = sums[i, 0], sums[i, 1]
+        by_w = by_w[0:8] + by_w[8:16] + by_w[16:24]
+        by_s = by_s[0:8] + by_s[8:16] + by_s[16:24]
+        row = lax.broadcasted_iota(jnp.int32, by_s.shape, 0)
+        terms = by_w + pltpu.roll(jnp.where(row < 4, -3.0 * by_s, 0.0), 4, 0)
         for pair in range(share // 2):
             place = i * (share // 2) + pair
             partial[place] = terms[:, pair * LANES:(pair + 1) * LANES]
@@ -299,33 +296,35 @@
     def pair_round(n, final):
         get_cross(n, tile_of(0), 0)
 
-        def two_tiles(pair, carry):
-            for side in range(2):
-                j = 2 * pair + side
-                i, after = tile_of(j), tile_of(j + 1)
-                before = tile_of(j + tiles - 1) if side else jnp.where(j > 0, tile_of(j + tiles - 1), tiles)
-                found = []
-                for b in range(blocks):
-                    if b < blocks - 1:
-                        get_cross(n, i, b + 1)
-                    else:
-                        get_cross(n, after, 0)
-                    weigh(n, i, b, side)
-                    if b < 2:
-                        found.append(gain(n, 1 - side, b))
-                add(before, *found)
-                if final and side:
+        def slot_tile(j, carry):
+            i = tile_of(j)
+            before = jnp.where(j > 0, tile_of(j + tiles - 1), tiles)
+            for b in range(blocks):
+                if b < blocks - 1:
+                    get_cross(n, i, b + 1)
+                else:
+                    get_cross(n, tile_of(j + 1), 0)
+                weigh(n, i, b)
+                if b == 0:
+                    gain(n, before, blocks - 1)
+                else:
+                    gain(n, i, b - 1)
+            if final:
+
+                @pl.when(j > 0)
+                def _():
                     finish(before)
-                elif final:
-
-                    @pl.when(j > 0)
-                    def _():
-                        finish(before)
+
+            else:
+
+                @pl.when((n == 0) & (j == 1) & (z // 2 % 2 == 0))
+                def _():
+                    lax.fori_loop(z // 4 * 4 + 2, z // 4 * 4 + 4, send_higher, 0)
 
             return carry
 
-        lax.fori_loop(0, tiles // 2, two_tiles, 0)
-        add(tile_of(tiles - 1), gain(n, 1, 0), gain(n, 1, 1))
+        lax.fori_loop(0, tiles, slot_tile, 0)
+        gain(n, tile_of(tiles - 1), blocks - 1)
         if final:
             finish(tile_of(tiles - 1))
 
@@ -334,7 +333,7 @@
 
         @pl.when(n == 0)
         def _():
-            lax.fori_loop(z + 2 - z % 2, lines, send_higher, 0)
+            lax.fori_loop(z // 4 * 4 + 4, lines, send_higher, 0)
 
         for k in (2 * n + 2, 2 * n + 3):
             block = line_peer(k)
@@ -407,14 +406,14 @@
             pltpu.VMEM((group, 8, LANES), F32),
             pltpu.VMEM((group, 8, LANES), F32),
             pltpu.VMEM((group // 2, 8, LANES), F32),
-            pltpu.VMEM((3, group * slots, LANES), F32),
-            pltpu.VMEM((group * slots, KDIM), BF16),
-            pltpu.VMEM((8, lines * stars), F32),
-            pltpu.VMEM((KDIM, lines * stars), BF16),
-            pltpu.VMEM((2 * lines * stars, LANES), BF16),
+            pltpu.VMEM((3, lines * stars, LANES), F32),
+            pltpu.VMEM((lines * stars, KDIM), BF16),
+            pltpu.VMEM((8, group * slots), F32),
+            pltpu.VMEM((KDIM, group * slots), BF16),
+            pltpu.VMEM((SOURCES, lines * stars), BF16),
             pltpu.VMEM((blocks, TILE, TILE), F32),
-            pltpu.VMEM((2, 2, TILE, 2 * blocks * TILE), BF16),
-            pltpu.VMEM((tiles + 1, TILE, LANES), F32),
+            pltpu.VMEM((blocks, 2, 2 * TILE, TILE), BF16),
+            pltpu.VMEM((tiles + 1, 2, SOURCES, TILE), F32),
             pltpu.SemaphoreType.DMA((7,)),
             pltpu.SemaphoreType.REGULAR((lines,)),
             pltpu.SemaphoreType.DMA((lines,)),

time: 66.2 us -> 53.1 us (0.80)
  Pallas kernels: 64.7 us -> 51.6 us
    pallas_call x1, Pallas kernels: 63.4 us -> 50.3 us  [body(): pl.pallas_call(functools.partial(kernel, lines, planes), out_shape=jax.Sh...]
where the time goes in v3:
time: 53.1 us; the launch traced here: 52.9 us
  Pallas kernels  51.6 us (97%)
  between operations  1.29 us (2%)
    pallas_call x1, Pallas kernels, body(): pl.pallas_call(functools.partial(kernel, lines, planes), out_shape=jax.Sh...  50.3 us
    pallas_call x1, Pallas kernels, body(): pl.pallas_call(correct_kernel, out_shape=(three,) * 4, in_specs=[pl.Block...  1.33 us

profile of v3, /device:TPU:224, one launch (start us, length us, event | category | flops | bytes accessed | tf_op | source)
XLA Modules:
  0.0 52.9 jit_solution(11805680507472654325)
XLA Ops:
  1.3 50.3 %forces.1.result = f32[24,64]{1,0:T(8,128)} custom-call(f32[3,384]{1,0:T(4,128)} %pos_hbm.1, f32[3,384]{1,0:T(4,128)} %vel_hbm.1, f32[3,384]{1,0:T(4,128)} %acc_hbm.1, f32[3,384]{1,0:T(4,128)} %jerk_hbm.1, f32[384]{0:T(512)} %mass_hbm.1, s32[384]{0:T(512)} %level_hbm.1, s32[1,64]{1,0:T(1,128)} %index_hbm.1), custom_call_target="tpu_custom_call" | custom-call | tf_op jit(solution)/shard_map/forces/pallas_call | solution.py:391
  51.5 1.3 %correct.1 = (f32[3,64]{1,0:T(4,128)}, f32[3,64]{1,0:T(4,128)}, f32[3,64]{1,0:T(4,128)}, f32[3,64]{1,0:T(4,128)}) custom-call(f32[24,64]{1,0:T(8,128)} %forces.1.result, s32[1]{0:T(128)S(6)} %copy.12.count), custom_call_target="tpu_custom_call" | custom-call | tf_op jit(solution)/shard_map/correct/pallas_call | solution.py:430

commit v4 on v3

--- a/solution.py
+++ b/solution.py
@@ -136,7 +136,9 @@
         return carry
 
     lax.fori_loop(0, group - 1, greet_plane, 0)
-    lax.fori_loop(z + 1, lines, greet_line, 0)
+    mate = line_peer(1)
+    greet_line(mate, 0)
+    lax.fori_loop(z // 2 * 2 + 2, lines, greet_line, 0)
     for load in loads:
         load.wait()
 
@@ -163,7 +165,7 @@
     actives[me, 0:3, 0:slots] = slot_pos
     actives[me, 3:6, 0:slots] = slot_vel
 
-    pl.semaphore_wait(barrier, group - 1 + z)
+    pl.semaphore_wait(barrier, group + z // 2 * 2)
 
     def line_copy(block, other):
         return pltpu.make_async_remote_copy(
@@ -201,7 +203,8 @@
         return carry
 
     lax.fori_loop(0, group - 1, send_plane, 0)
-    lax.fori_loop(0, z, send_lower, 0)
+    line_copy(z, mate).start()
+    lax.fori_loop(0, z // 2 * 2, send_lower, 0)
 
     def take_stars(k, block):
         tile = fields[block]
@@ -231,12 +234,8 @@
 
     lax.fori_loop(0, group // 2, take_slots, 0)
 
-    @pl.when(z % 2 == 0)
-    def _():
-        send_higher(z + 1, 0)
-
-    line_copy(line_peer(1), line_peer(1)).wait_recv()
-    take_stars(1, line_peer(1))
+    line_copy(mate, mate).wait_recv()
+    take_stars(1, mate)
 
     blocks = 2 * stars // TILE
     rounds = lines // 2
@@ -247,10 +246,12 @@
     def slots_of(i):
         return pl.ds(pl.multiple_of(i * TILE, TILE), TILE)
 
-    def get_cross(n, i, b):
-        cross[b] = jnp.dot(left[stars_of(n, b), :], along[:, slots_of(i)], preferred_element_type=F32)
-
-    def weigh(n, i, b):
+    def get_cross(n, i, b, part):
+        half = slice(part * TILE // 2, (part + 1) * TILE // 2)
+        rows = pl.ds(pl.multiple_of((n * blocks + b) * TILE + part * TILE // 2, TILE // 2), TILE // 2)
+        cross[b, half, :] = jnp.dot(left[rows, :], along[:, slots_of(i)], preferred_element_type=F32)
+
+    def weigh(n, i, b, beside):
         state = [jnp.broadcast_to(place_rows[c:c + 1, slots_of(i)], (ROWS, TILE)) for c in range(3)]
         for sub in range(0, TILE, ROWS):
             rows = pl.ds(pl.multiple_of((n * blocks + b) * TILE + sub, ROWS), ROWS)
@@ -265,12 +266,12 @@
                 high = value.astype(BF16)
                 high_low[b, kind, sub:sub + ROWS, :] = high
                 high_low[b, kind, TILE + sub:TILE + sub + ROWS, :] = (value - high.astype(F32)).astype(BF16)
-
-    def gain(n, i, b):
-        source = moments[:, stars_of(n, b)]
-        source = jnp.concatenate([source, source], 1)
-        for kind in range(2):
-            sums[i, kind] += jnp.dot(source, high_low[b, kind], preferred_element_type=F32)
+            if sub // ROWS in beside:
+                beside[sub // ROWS]()
+
+    def gain(n, i, b, kind, part):
+        piece = high_low[b, kind, part * TILE:(part + 1) * TILE, :]
+        sums[i, kind] += jnp.dot(moments[:, stars_of(n, b)], piece, preferred_element_type=F32)
 
     def finish(i):
         by_w, by_s = sums[i, 0], sums[i, 1]
@@ -294,21 +295,21 @@
     sums[...] = jnp.zeros_like(sums)
 
     def pair_round(n, final):
-        get_cross(n, tile_of(0), 0)
+        for part in range(2):
+            get_cross(n, tile_of(0), 0, part)
 
         def slot_tile(j, carry):
             i = tile_of(j)
             before = jnp.where(j > 0, tile_of(j + tiles - 1), tiles)
             for b in range(blocks):
-                if b < blocks - 1:
-                    get_cross(n, i, b + 1)
-                else:
-                    get_cross(n, tile_of(j + 1), 0)
-                weigh(n, i, b)
-                if b == 0:
-                    gain(n, before, blocks - 1)
-                else:
-                    gain(n, i, b - 1)
+                done = (before, blocks - 1) if b == 0 else (i, b - 1)
+                soon = (i, b + 1) if b < blocks - 1 else (tile_of(j + 1), 0)
+                beside = {}
+                for part in range(2):
+                    beside[8 * part + 3] = functools.partial(get_cross, n, *soon, part)
+                    for kind in range(2):
+                        beside[8 * part + 4 * kind + 1] = functools.partial(gain, n, *done, kind, part)
+                weigh(n, i, b, beside)
             if final:
 
                 @pl.when(j > 0)
@@ -323,8 +324,10 @@
 
             return carry
 
-        lax.fori_loop(0, tiles, slot_tile, 0)
-        gain(n, tile_of(tiles - 1), blocks - 1)
+        lax.fori_loop(0, tiles, slot_tile, 0, unroll=1 if final else 2)
+        for kind in range(2):
+            for part in range(2):
+                gain(n, tile_of(tiles - 1), blocks - 1, kind, part)
         if final:
             finish(tile_of(tiles - 1))
 

time: 53.1 us -> 51.1 us (0.962); the launches traced: 52.9 us -> 50.3 us
  Pallas kernels: 51.6 us -> 49 us
    pallas_call x1, Pallas kernels: 50.3 us -> 47.6 us  [body(): pl.pallas_call(functools.partial(kernel, lines, planes), out_shape=jax.Sh...]
where the time goes in v4:
time: 51.1 us; the launch traced here: 50.3 us
  Pallas kernels  49 us (96%)
  between operations  1.29 us (3%)
    pallas_call x1, Pallas kernels, body(): pl.pallas_call(functools.partial(kernel, lines, planes), out_shape=jax.Sh...  47.6 us
    pallas_call x1, Pallas kernels, body(): pl.pallas_call(correct_kernel, out_shape=(three,) * 4, in_specs=[pl.Block...  1.33 us

profile of v4, /device:TPU:224, one launch (start us, length us, event | category | flops | bytes accessed | tf_op | source)
XLA Modules:
  0.0 50.3 jit_solution(7869149888880564954)
XLA Ops:
  1.3 47.6 %forces.1.result = f32[24,64]{1,0:T(8,128)} custom-call(f32[3,384]{1,0:T(4,128)} %pos_hbm.1, f32[3,384]{1,0:T(4,128)} %vel_hbm.1, f32[3,384]{1,0:T(4,128)} %acc_hbm.1, f32[3,384]{1,0:T(4,128)} %jerk_hbm.1, f32[384]{0:T(512)} %mass_hbm.1, s32[384]{0:T(512)} %level_hbm.1, s32[1,64]{1,0:T(1,128)} %index_hbm.1), custom_call_target="tpu_custom_call" | custom-call | tf_op jit(solution)/shard_map/forces/pallas_call | solution.py:394
  48.9 1.3 %correct.1 = (f32[3,64]{1,0:T(4,128)}, f32[3,64]{1,0:T(4,128)}, f32[3,64]{1,0:T(4,128)}, f32[3,64]{1,0:T(4,128)}) custom-call(f32[24,64]{1,0:T(8,128)} %forces.1.result, s32[1]{0:T(128)S(6)} %copy.12.count), custom_call_target="tpu_custom_call" | custom-call | tf_op jit(solution)/shard_map/correct/pallas_call | solution.py:433

commit v5 on v4

--- a/solution.py
+++ b/solution.py
@@ -15,6 +15,7 @@
 LANES = 128
 TILE = 256
 KDIM = 128
+STATE_ROW = 88
 ROWS = 16
 SOURCES = 32
 VMEM_LIMIT = 63 * 1024 * 1024
@@ -64,7 +65,7 @@
     none = jnp.zeros((3, width), F32)
     own = jnp.concatenate(own_cross(grid, near, far) + [none], 0)
     other = jnp.concatenate([jnp.ones((5, width), F32), none], 0)
-    pad = jnp.zeros((KDIM - 88, width), F32)
+    pad = jnp.zeros((KDIM - STATE_ROW, width), F32)
     return jnp.concatenate([grid] * 3 + [near] * 3 + [far] * 3 + [own, other, pad], 0)
 
 
@@ -75,8 +76,8 @@
     crossed = [jnp.concatenate([-part[3:6], -part[0:3], part[6:8]], 0) for part in (grid, near, far)]
     other = jnp.concatenate([jnp.ones((5, width), F32), none], 0)
     own = jnp.concatenate(own_cross(grid, near, far) + [none], 0)
-    pad = jnp.zeros((KDIM - 88, width), F32)
-    return jnp.concatenate(crossed * 3 + [other, own, pad], 0)
+    pad = jnp.zeros((KDIM - STATE_ROW - 8, width), F32)
+    return jnp.concatenate(crossed * 3 + [other, own, tile, pad], 0)
 
 
 def source_rows(tile):
@@ -135,7 +136,7 @@
         pl.semaphore_signal(barrier, inc=1, device_id=plane_id(plane_peer(k)), device_id_type=MESH)
         return carry
 
-    lax.fori_loop(0, group - 1, greet_plane, 0)
+    lax.fori_loop(0, group - 1, greet_plane, 0, unroll=True)
     mate = line_peer(1)
     greet_line(mate, 0)
     lax.fori_loop(z // 2 * 2 + 2, lines, greet_line, 0)
@@ -202,17 +203,17 @@
         plane_copy(me, plane_peer(k), k).start()
         return carry
 
-    lax.fori_loop(0, group - 1, send_plane, 0)
+    lax.fori_loop(0, group - 1, send_plane, 0, unroll=True)
     line_copy(z, mate).start()
     lax.fori_loop(0, z // 2 * 2, send_lower, 0)
 
     def take_stars(k, block):
         tile = fields[block]
         at = pl.ds(pl.multiple_of(k * stars, LANES), stars)
-        left[at, :] = star_rows(tile).T.astype(BF16)
-        turned = jnp.concatenate([tile] + [jnp.zeros_like(tile)] * 15, 0).T
+        turned = star_rows(tile).T
+        left[at, :] = turned.astype(BF16)
         for c in range(3):
-            spread[c, at, :] = jnp.broadcast_to(turned[:, c:c + 1], (stars, LANES))
+            spread[c, at, :] = jnp.broadcast_to(turned[:, STATE_ROW + c:STATE_ROW + c + 1], (stars, LANES))
         moments[:, at] = source_rows(tile).astype(BF16)
 
     take_stars(0, z)
@@ -221,7 +222,7 @@
         plane_copy(plane_peer(k), plane_peer(k), k).wait_recv()
         return carry
 
-    lax.fori_loop(0, group - 1, get_plane, 0)
+    lax.fori_loop(0, group - 1, get_plane, 0, unroll=True)
 
     lane = lax.broadcasted_iota(jnp.int32, (8, LANES), 1)
 
@@ -232,7 +233,7 @@
         along[:, at] = slot_rows(tile).astype(BF16)
         return carry
 
-    lax.fori_loop(0, group // 2, take_slots, 0)
+    lax.fori_loop(0, group // 2, take_slots, 0, unroll=True)
 
     line_copy(mate, mate).wait_recv()
     take_stars(1, mate)
@@ -349,6 +350,16 @@
 
     arrived[me] = partial[me // 2]
 
+    def get_part(k, carry):
+        other = plane_peer(k)
+        part_copy(other // 2, other, other).wait_recv()
+        return carry
+
+    lax.fori_loop(0, group - 1, get_part, 0, unroll=True)
+    terms = jnp.sum(arrived[...], axis=0)
+    terms = jnp.where(me % 2 == 0, terms, pltpu.roll(terms, slots, 1))
+    result[0:8, :] = terms[:, 0:slots]
+
     def end_line(k, carry):
         line_copy(z, line_peer(k + 1)).wait_send()
         return carry
@@ -357,14 +368,10 @@
         other = plane_peer(k)
         plane_copy(me, other, k).wait_send()
         part_copy(other // 2, me, other).wait_send()
-        part_copy(other // 2, other, other).wait_recv()
-        return carry
-
-    lax.fori_loop(0, lines - 1, end_line, 0)
-    lax.fori_loop(0, group - 1, end_plane, 0)
-    terms = jnp.sum(arrived[...], axis=0)
-    terms = jnp.where(me % 2 == 0, terms, pltpu.roll(terms, slots, 1))
-    result[0:8, :] = terms[:, 0:slots]
+        return carry
+
+    lax.fori_loop(0, lines - 1, end_line, 0, unroll=True)
+    lax.fori_loop(0, group - 1, end_plane, 0, unroll=True)
 
 
 def correct_kernel(result, count, pos_hbm, vel_hbm, acc_hbm, jerk_hbm, pos, vel, acc, jerk, store_sem):

time: 51.1 us -> 49 us (0.959)
  Pallas kernels: 49 us -> 47 us
    pallas_call x1, Pallas kernels: 47.6 us -> 45.7 us  [body(): pl.pallas_call(functools.partial(kernel, lines, planes), out_shape=jax.Sh...]
where the time goes in v5:
time: 49 us; the launch traced here: 48.3 us
  Pallas kernels  47 us (96%)
  between operations  1.29 us (3%)
    pallas_call x1, Pallas kernels, body(): pl.pallas_call(functools.partial(kernel, lines, planes), out_shape=jax.Sh...  45.7 us
    pallas_call x1, Pallas kernels, body(): pl.pallas_call(correct_kernel, out_shape=(three,) * 4, in_specs=[pl.Block...  1.33 us

profile of v5, /device:TPU:224, one launch (start us, length us, event | category | flops | bytes accessed | tf_op | source)
XLA Modules:
  0.0 48.3 jit_solution(1266267772085542298)
XLA Ops:
  1.3 45.7 %forces.1.result = f32[24,64]{1,0:T(8,128)} custom-call(f32[3,384]{1,0:T(4,128)} %pos_hbm.1, f32[3,384]{1,0:T(4,128)} %vel_hbm.1, f32[3,384]{1,0:T(4,128)} %acc_hbm.1, f32[3,384]{1,0:T(4,128)} %jerk_hbm.1, f32[384]{0:T(512)} %mass_hbm.1, s32[384]{0:T(512)} %level_hbm.1, s32[1,64]{1,0:T(1,128)} %index_hbm.1), custom_call_target="tpu_custom_call" | custom-call | tf_op jit(solution)/shard_map/forces/pallas_call | solution.py:401
  47.0 1.3 %correct.1 = (f32[3,64]{1,0:T(4,128)}, f32[3,64]{1,0:T(4,128)}, f32[3,64]{1,0:T(4,128)}, f32[3,64]{1,0:T(4,128)}) custom-call(f32[24,64]{1,0:T(8,128)} %forces.1.result, s32[1]{0:T(128)S(6)} %copy.12.count), custom_call_target="tpu_custom_call" | custom-call | tf_op jit(solution)/shard_map/correct/pallas_call | solution.py:440

commit v6 on v5

--- a/solution.py
+++ b/solution.py
@@ -14,6 +14,7 @@
 BF16 = jnp.bfloat16
 LANES = 128
 TILE = 256
+WIDE = 1024
 KDIM = 128
 STATE_ROW = 88
 ROWS = 16
@@ -95,8 +96,9 @@
 ):
     group = 2 * planes
     stars, slots = pos.shape[1], index.shape[1]
-    tiles = group * slots // TILE
-    share = TILE // slots
+    wide_tile = sums.shape[3]
+    tiles = group * slots // wide_tile
+    share = wide_tile // slots
     wide, s = lax.axis_index("wide"), lax.axis_index("sum")
     z, core = wide // 2, wide % 2
     me = core * planes + s
@@ -245,7 +247,7 @@
         return pl.ds(pl.multiple_of((n * blocks + b) * TILE, TILE), TILE)
 
     def slots_of(i):
-        return pl.ds(pl.multiple_of(i * TILE, TILE), TILE)
+        return pl.ds(pl.multiple_of(i * wide_tile, wide_tile), wide_tile)
 
     def get_cross(n, i, b, part):
         half = slice(part * TILE // 2, (part + 1) * TILE // 2)
@@ -253,22 +255,27 @@
         cross[b, half, :] = jnp.dot(left[rows, :], along[:, slots_of(i)], preferred_element_type=F32)
 
     def weigh(n, i, b, beside):
-        state = [jnp.broadcast_to(place_rows[c:c + 1, slots_of(i)], (ROWS, TILE)) for c in range(3)]
-        for sub in range(0, TILE, ROWS):
-            rows = pl.ds(pl.multiple_of((n * blocks + b) * TILE + sub, ROWS), ROWS)
-            star = [jnp.concatenate([spread[c, rows, :]] * (TILE // LANES), 1) for c in range(3)]
-            r = [star[c] - state[c] for c in range(3)]
-            q = r[0] * r[0] + r[1] * r[1] + (r[2] * r[2] + SOFT2)
-            inverse = lax.rsqrt(q)
-            inverse2 = inverse * inverse
-            w = inverse2 * inverse
-            sw = (w * inverse2) * cross[b, sub:sub + ROWS, :]
-            for kind, value in enumerate((w, sw)):
-                high = value.astype(BF16)
-                high_low[b, kind, sub:sub + ROWS, :] = high
-                high_low[b, kind, TILE + sub:TILE + sub + ROWS, :] = (value - high.astype(F32)).astype(BF16)
-            if sub // ROWS in beside:
-                beside[sub // ROWS]()
+        step = 0
+        for lanes in range(0, wide_tile, TILE):
+            cols = pl.ds(pl.multiple_of(i * wide_tile + lanes, TILE), TILE)
+            state = [jnp.broadcast_to(place_rows[c:c + 1, cols], (ROWS, TILE)) for c in range(3)]
+            for sub in range(0, TILE, ROWS):
+                rows = pl.ds(pl.multiple_of((n * blocks + b) * TILE + sub, ROWS), ROWS)
+                star = [jnp.concatenate([spread[c, rows, :]] * (TILE // LANES), 1) for c in range(3)]
+                r = [star[c] - state[c] for c in range(3)]
+                q = r[0] * r[0] + r[1] * r[1] + (r[2] * r[2] + SOFT2)
+                inverse = lax.rsqrt(q)
+                inverse2 = inverse * inverse
+                w = inverse2 * inverse
+                sw = (w * inverse2) * cross[b, sub:sub + ROWS, lanes:lanes + TILE]
+                for kind, value in enumerate((w, sw)):
+                    high = value.astype(BF16)
+                    low = (value - high.astype(F32)).astype(BF16)
+                    high_low[b, kind, sub:sub + ROWS, lanes:lanes + TILE] = high
+                    high_low[b, kind, TILE + sub:TILE + sub + ROWS, lanes:lanes + TILE] = low
+                if step in beside:
+                    beside[step]()
+                step += 1
 
     def gain(n, i, b, kind, part):
         piece = high_low[b, kind, part * TILE:(part + 1) * TILE, :]
@@ -306,10 +313,11 @@
                 done = (before, blocks - 1) if b == 0 else (i, b - 1)
                 soon = (i, b + 1) if b < blocks - 1 else (tile_of(j + 1), 0)
                 beside = {}
+                steps = wide_tile // ROWS
                 for part in range(2):
-                    beside[8 * part + 3] = functools.partial(get_cross, n, *soon, part)
+                    beside[part * steps // 2 + steps * 3 // 8] = functools.partial(get_cross, n, *soon, part)
                     for kind in range(2):
-                        beside[8 * part + 4 * kind + 1] = functools.partial(gain, n, *done, kind, part)
+                        beside[part * steps // 2 + kind * steps // 4 + steps // 16] = functools.partial(gain, n, *done, kind, part)
                 weigh(n, i, b, beside)
             if final:
 
@@ -319,13 +327,13 @@
 
             else:
 
-                @pl.when((n == 0) & (j == 1) & (z // 2 % 2 == 0))
+                @pl.when((n == 0) & (j == 0) & (z // 2 % 2 == 0))
                 def _():
                     lax.fori_loop(z // 4 * 4 + 2, z // 4 * 4 + 4, send_higher, 0)
 
             return carry
 
-        lax.fori_loop(0, tiles, slot_tile, 0, unroll=1 if final else 2)
+        lax.fori_loop(0, tiles, slot_tile, 0)
         for kind in range(2):
             for part in range(2):
                 gain(n, tile_of(tiles - 1), blocks - 1, kind, part)
@@ -397,7 +405,8 @@
 def body(lines, planes, pos, vel, acc, jerk, masses, levels, index, count):
     stars, slots, group = pos.shape[1], index.shape[1], 2 * planes
     hbm = pl.BlockSpec(memory_space=pl.ANY)
-    tiles, blocks = group * slots // TILE, 2 * stars // TILE
+    wide_tile, blocks = min(WIDE, group * slots), 2 * stars // TILE
+    tiles = group * slots // wide_tile
     result = pl.pallas_call(
         functools.partial(kernel, lines, planes),
         out_shape=jax.ShapeDtypeStruct((24, slots), F32),
@@ -421,9 +430,9 @@
             pltpu.VMEM((8, group * slots), F32),
             pltpu.VMEM((KDIM, group * slots), BF16),
             pltpu.VMEM((SOURCES, lines * stars), BF16),
-            pltpu.VMEM((blocks, TILE, TILE), F32),
-            pltpu.VMEM((blocks, 2, 2 * TILE, TILE), BF16),
-            pltpu.VMEM((tiles + 1, 2, SOURCES, TILE), F32),
+            pltpu.VMEM((blocks, TILE, wide_tile), F32),
+            pltpu.VMEM((blocks, 2, 2 * TILE, wide_tile), BF16),
+            pltpu.VMEM((tiles + 1, 2, SOURCES, wide_tile), F32),
             pltpu.SemaphoreType.DMA((7,)),
             pltpu.SemaphoreType.REGULAR((lines,)),
             pltpu.SemaphoreType.DMA((lines,)),

time: 49 us -> 51.3 us (1.047)
  Pallas kernels: 47 us -> 49.6 us
    pallas_call x1, Pallas kernels: 45.7 us -> 48.2 us  [body(): pl.pallas_call(functools.partial(kernel, lines, planes), out_shape=jax.Sh...]
where the time goes in v6:
time: 51.3 us; the launch traced here: 50.9 us
  Pallas kernels  49.6 us (97%)
  between operations  1.29 us (3%)
    pallas_call x1, Pallas kernels, body(): pl.pallas_call(functools.partial(kernel, lines, planes), out_shape=jax.Sh...  48.2 us
    pallas_call x1, Pallas kernels, body(): pl.pallas_call(correct_kernel, out_shape=(three,) * 4, in_specs=[pl.Block...  1.33 us

profile of v6, /device:TPU:224, one launch (start us, length us, event | category | flops | bytes accessed | tf_op | source)
XLA Modules:
  0.0 50.9 jit_solution(13771226986622474642)
XLA Ops:
  1.3 48.2 %forces.1.result = f32[24,64]{1,0:T(8,128)} custom-call(f32[3,384]{1,0:T(4,128)} %pos_hbm.1, f32[3,384]{1,0:T(4,128)} %vel_hbm.1, f32[3,384]{1,0:T(4,128)} %acc_hbm.1, f32[3,384]{1,0:T(4,128)} %jerk_hbm.1, f32[384]{0:T(512)} %mass_hbm.1, s32[384]{0:T(512)} %level_hbm.1, s32[1,64]{1,0:T(1,128)} %index_hbm.1), custom_call_target="tpu_custom_call" | custom-call | tf_op jit(solution)/shard_map/forces/pallas_call | solution.py:410
  49.5 1.3 %correct.1 = (f32[3,64]{1,0:T(4,128)}, f32[3,64]{1,0:T(4,128)}, f32[3,64]{1,0:T(4,128)}, f32[3,64]{1,0:T(4,128)}) custom-call(f32[24,64]{1,0:T(8,128)} %forces.1.result, s32[1]{0:T(128)S(6)} %copy.12.count), custom_call_target="tpu_custom_call" | custom-call | tf_op jit(solution)/shard_map/correct/pallas_call | solution.py:449

commit v7 on v5

--- a/solution.py
+++ b/solution.py
@@ -15,7 +15,6 @@
 LANES = 128
 TILE = 256
 KDIM = 128
-STATE_ROW = 88
 ROWS = 16
 SOURCES = 32
 VMEM_LIMIT = 63 * 1024 * 1024
@@ -51,33 +50,61 @@
     return grid, near, far
 
 
-def own_cross(grid, near, far):
+def own_terms(grid, near, far):
     small = near + far
     gp, gv, sp, sv = grid[0:3], grid[3:6], small[0:3], small[3:6]
-    cross = jnp.sum(gp * gv, axis=0, keepdims=True)
-    rest = jnp.sum(gp * sv + sp * gv + sp * sv, axis=0, keepdims=True)
-    return list(pieces(cross)[:2] + pieces(rest))
+
+    def total(value):
+        return jnp.sum(value, axis=0, keepdims=True)
+
+    square, square_rest = total(gp * gp), total(2.0 * gp * sp + sp * sp) + 0.5 * SOFT2
+    cross, cross_rest = total(gp * gv), total(gp * sv + sp * gv + sp * sv)
+    return list(pieces(square)[:2]), list(pieces(square_rest)), list(pieces(cross)[:2] + pieces(cross_rest))
+
+
+def star_rows(tile):
+    width = tile.shape[1]
+    grid, near, far = split_state(tile)
+    square, square_rest, cross = own_terms(grid, near, far)
+
+    def ones(count):
+        return jnp.ones((count, width), F32)
+
+    first = jnp.concatenate([grid[0:3]] + square + [ones(2), jnp.zeros((1, width), F32)], 0)
+    second = jnp.concatenate([grid[3:6]] + cross, 0)
+    third = jnp.concatenate([ones(5)] + square_rest, 0)
+    pad = jnp.zeros((KDIM - 88, width), F32)
+    return jnp.concatenate([first, second, third] + [grid] * 2 + [near] * 3 + [far] * 3 + [pad], 0)
 
 
 def slot_rows(tile):
     width = tile.shape[1]
     grid, near, far = split_state(tile)
-    none = jnp.zeros((3, width), F32)
-    own = jnp.concatenate(own_cross(grid, near, far) + [none], 0)
-    other = jnp.concatenate([jnp.ones((5, width), F32), none], 0)
-    pad = jnp.zeros((KDIM - STATE_ROW, width), F32)
-    return jnp.concatenate([grid] * 3 + [near] * 3 + [far] * 3 + [own, other, pad], 0)
-
-
-def star_rows(tile):
-    width = tile.shape[1]
-    grid, near, far = split_state(tile)
-    none = jnp.zeros((3, width), F32)
-    crossed = [jnp.concatenate([-part[3:6], -part[0:3], part[6:8]], 0) for part in (grid, near, far)]
-    other = jnp.concatenate([jnp.ones((5, width), F32), none], 0)
-    own = jnp.concatenate(own_cross(grid, near, far) + [none], 0)
-    pad = jnp.zeros((KDIM - STATE_ROW - 8, width), F32)
-    return jnp.concatenate(crossed * 3 + [other, own, tile, pad], 0)
+    square, square_rest, cross = own_terms(grid, near, far)
+    row = lax.broadcasted_iota(jnp.int32, tile.shape, 0)
+
+    def ones(count):
+        return jnp.ones((count, width), F32)
+
+    def none(count):
+        return jnp.zeros((count, width), F32)
+
+    def for_square(part):
+        return jnp.where(row < 3, -2.0 * part, 0.0)
+
+    def for_cross(part):
+        return jnp.concatenate([-part[3:6], -part[0:3], part[6:8]], 0)
+
+    first = jnp.concatenate([-2.0 * grid[0:3], ones(2)] + square + [none(1)], 0)
+    third = jnp.concatenate(square_rest + [none(2), ones(3)], 0)
+    parts = (near, far) + (grid, near, far) * 2
+    pad = none(KDIM - 88)
+    in_square = jnp.concatenate([first, none(8), third] + [for_square(part) for part in parts] + [pad], 0)
+    first = jnp.concatenate([-grid[3:6], none(5)], 0)
+    second = jnp.concatenate([-grid[0:3], ones(5)], 0)
+    third = jnp.concatenate(cross + [none(3)], 0)
+    in_cross = jnp.concatenate([first, second, third] + [for_cross(part) for part in parts] + [pad], 0)
+    return in_square, in_cross
 
 
 def source_rows(tile):
@@ -90,7 +117,7 @@
 def kernel(
     lines, planes, pos_hbm, vel_hbm, acc_hbm, jerk_hbm, mass_hbm, level_hbm, index_hbm, result,
     pos, vel, acc, jerk, mass, level, index, stage, fields, actives, arrived, partial,
-    spread, left, place_rows, along, moments, cross, high_low, sums,
+    left, along, moments, both, high_low, sums,
     load_sem, ready, field_send, field_recv, active_send, active_recv, part_send, part_recv,
 ):
     group = 2 * planes
@@ -210,10 +237,7 @@
     def take_stars(k, block):
         tile = fields[block]
         at = pl.ds(pl.multiple_of(k * stars, LANES), stars)
-        turned = star_rows(tile).T
-        left[at, :] = turned.astype(BF16)
-        for c in range(3):
-            spread[c, at, :] = jnp.broadcast_to(turned[:, STATE_ROW + c:STATE_ROW + c + 1], (stars, LANES))
+        left[at, :] = star_rows(tile).T.astype(BF16)
         moments[:, at] = source_rows(tile).astype(BF16)
 
     take_stars(0, z)
@@ -228,9 +252,9 @@
 
     def take_slots(pair, carry):
         tile = jnp.where(lane < slots, actives[2 * pair], pltpu.roll(actives[2 * pair + 1], slots, 1))
-        at = pl.ds(pl.multiple_of(pair * LANES, LANES), LANES)
-        place_rows[:, at] = tile
-        along[:, at] = slot_rows(tile).astype(BF16)
+        start = pair * LANES // TILE * 2 * TILE + pair * LANES % TILE
+        for offset, value in zip((0, TILE), slot_rows(tile)):
+            along[:, pl.ds(pl.multiple_of(start + offset, LANES), LANES)] = value.astype(BF16)
         return carry
 
     lax.fori_loop(0, group // 2, take_slots, 0, unroll=True)
@@ -244,25 +268,18 @@
     def stars_of(n, b):
         return pl.ds(pl.multiple_of((n * blocks + b) * TILE, TILE), TILE)
 
-    def slots_of(i):
-        return pl.ds(pl.multiple_of(i * TILE, TILE), TILE)
-
-    def get_cross(n, i, b, part):
+    def relate(n, i, b, part):
         half = slice(part * TILE // 2, (part + 1) * TILE // 2)
         rows = pl.ds(pl.multiple_of((n * blocks + b) * TILE + part * TILE // 2, TILE // 2), TILE // 2)
-        cross[b, half, :] = jnp.dot(left[rows, :], along[:, slots_of(i)], preferred_element_type=F32)
-
-    def weigh(n, i, b, beside):
-        state = [jnp.broadcast_to(place_rows[c:c + 1, slots_of(i)], (ROWS, TILE)) for c in range(3)]
+        cols = pl.ds(pl.multiple_of(i * 2 * TILE, 2 * TILE), 2 * TILE)
+        both[b, half, :] = jnp.dot(left[rows, :], along[:, cols], preferred_element_type=F32)
+
+    def weigh(b, beside):
         for sub in range(0, TILE, ROWS):
-            rows = pl.ds(pl.multiple_of((n * blocks + b) * TILE + sub, ROWS), ROWS)
-            star = [jnp.concatenate([spread[c, rows, :]] * (TILE // LANES), 1) for c in range(3)]
-            r = [star[c] - state[c] for c in range(3)]
-            q = r[0] * r[0] + r[1] * r[1] + (r[2] * r[2] + SOFT2)
-            inverse = lax.rsqrt(q)
+            inverse = lax.rsqrt(both[b, sub:sub + ROWS, 0:TILE])
             inverse2 = inverse * inverse
             w = inverse2 * inverse
-            sw = (w * inverse2) * cross[b, sub:sub + ROWS, :]
+            sw = (w * inverse2) * both[b, sub:sub + ROWS, TILE:2 * TILE]
             for kind, value in enumerate((w, sw)):
                 high = value.astype(BF16)
                 high_low[b, kind, sub:sub + ROWS, :] = high
@@ -297,7 +314,7 @@
 
     def pair_round(n, final):
         for part in range(2):
-            get_cross(n, tile_of(0), 0, part)
+            relate(n, tile_of(0), 0, part)
 
         def slot_tile(j, carry):
             i = tile_of(j)
@@ -307,10 +324,10 @@
                 soon = (i, b + 1) if b < blocks - 1 else (tile_of(j + 1), 0)
                 beside = {}
                 for part in range(2):
-                    beside[8 * part + 3] = functools.partial(get_cross, n, *soon, part)
+                    beside[8 * part + 3] = functools.partial(relate, n, *soon, part)
                     for kind in range(2):
                         beside[8 * part + 4 * kind + 1] = functools.partial(gain, n, *done, kind, part)
-                weigh(n, i, b, beside)
+                weigh(b, beside)
             if final:
 
                 @pl.when(j > 0)
@@ -416,12 +433,10 @@
             pltpu.VMEM((group, 8, LANES), F32),
             pltpu.VMEM((group, 8, LANES), F32),
             pltpu.VMEM((group // 2, 8, LANES), F32),
-            pltpu.VMEM((3, lines * stars, LANES), F32),
             pltpu.VMEM((lines * stars, KDIM), BF16),
-            pltpu.VMEM((8, group * slots), F32),
-            pltpu.VMEM((KDIM, group * slots), BF16),
+            pltpu.VMEM((KDIM, 2 * group * slots), BF16),
             pltpu.VMEM((SOURCES, lines * stars), BF16),
-            pltpu.VMEM((blocks, TILE, TILE), F32),
+            pltpu.VMEM((blocks, TILE, 2 * TILE), F32),
             pltpu.VMEM((blocks, 2, 2 * TILE, TILE), BF16),
             pltpu.VMEM((tiles + 1, 2, SOURCES, TILE), F32),
             pltpu.SemaphoreType.DMA((7,)),

time: 49 us -> 42.8 us (0.87)
  Pallas kernels: 47 us -> 40.8 us
    pallas_call x1, Pallas kernels: 45.7 us -> 39.5 us  [body(): pl.pallas_call(functools.partial(kernel, lines, planes), out_shape=jax.Sh...]
where the time goes in v7:
time: 42.8 us; the launch traced here: 42.1 us
  Pallas kernels  40.8 us (95%)
  between operations  1.29 us (3%)
    pallas_call x1, Pallas kernels, body(): pl.pallas_call(functools.partial(kernel, lines, planes), out_shape=jax.Sh...  39.5 us
    pallas_call x1, Pallas kernels, body(): pl.pallas_call(correct_kernel, out_shape=(three,) * 4, in_specs=[pl.Block...  1.33 us

profile of v7, /device:TPU:224, one launch (start us, length us, event | category | flops | bytes accessed | tf_op | source)
XLA Modules:
  0.0 42.1 jit_solution(8882534107592486080)
XLA Ops:
  1.3 39.5 %forces.1.result = f32[24,64]{1,0:T(8,128)} custom-call(f32[3,384]{1,0:T(4,128)} %pos_hbm.1, f32[3,384]{1,0:T(4,128)} %vel_hbm.1, f32[3,384]{1,0:T(4,128)} %acc_hbm.1, f32[3,384]{1,0:T(4,128)} %jerk_hbm.1, f32[384]{0:T(512)} %mass_hbm.1, s32[384]{0:T(512)} %level_hbm.1, s32[1,64]{1,0:T(1,128)} %index_hbm.1), custom_call_target="tpu_custom_call" | custom-call | tf_op jit(solution)/shard_map/forces/pallas_call | solution.py:418
  40.8 1.3 %correct.1 = (f32[3,64]{1,0:T(4,128)}, f32[3,64]{1,0:T(4,128)}, f32[3,64]{1,0:T(4,128)}, f32[3,64]{1,0:T(4,128)}) custom-call(f32[24,64]{1,0:T(8,128)} %forces.1.result, s32[1]{0:T(128)S(6)} %copy.12.count), custom_call_target="tpu_custom_call" | custom-call | tf_op jit(solution)/shard_map/correct/pallas_call | solution.py:455

commit v8 on v7

--- a/solution.py
+++ b/solution.py
@@ -117,7 +117,7 @@
 def kernel(
     lines, planes, pos_hbm, vel_hbm, acc_hbm, jerk_hbm, mass_hbm, level_hbm, index_hbm, result,
     pos, vel, acc, jerk, mass, level, index, stage, fields, actives, arrived, partial,
-    left, along, moments, both, high_low, sums,
+    left, along, moments, high_low, sums,
     load_sem, ready, field_send, field_recv, active_send, active_recv, part_send, part_recv,
 ):
     group = 2 * planes
@@ -268,18 +268,14 @@
     def stars_of(n, b):
         return pl.ds(pl.multiple_of((n * blocks + b) * TILE, TILE), TILE)
 
-    def relate(n, i, b, part):
-        half = slice(part * TILE // 2, (part + 1) * TILE // 2)
-        rows = pl.ds(pl.multiple_of((n * blocks + b) * TILE + part * TILE // 2, TILE // 2), TILE // 2)
+    def weigh(n, i, b, beside):
         cols = pl.ds(pl.multiple_of(i * 2 * TILE, 2 * TILE), 2 * TILE)
-        both[b, half, :] = jnp.dot(left[rows, :], along[:, cols], preferred_element_type=F32)
-
-    def weigh(b, beside):
+        both = jnp.dot(left[stars_of(n, b), :], along[:, cols], preferred_element_type=F32)
         for sub in range(0, TILE, ROWS):
-            inverse = lax.rsqrt(both[b, sub:sub + ROWS, 0:TILE])
+            inverse = lax.rsqrt(both[sub:sub + ROWS, 0:TILE])
             inverse2 = inverse * inverse
             w = inverse2 * inverse
-            sw = (w * inverse2) * both[b, sub:sub + ROWS, TILE:2 * TILE]
+            sw = (w * inverse2) * both[sub:sub + ROWS, TILE:2 * TILE]
             for kind, value in enumerate((w, sw)):
                 high = value.astype(BF16)
                 high_low[b, kind, sub:sub + ROWS, :] = high
@@ -313,21 +309,17 @@
     sums[...] = jnp.zeros_like(sums)
 
     def pair_round(n, final):
-        for part in range(2):
-            relate(n, tile_of(0), 0, part)
 
         def slot_tile(j, carry):
             i = tile_of(j)
             before = jnp.where(j > 0, tile_of(j + tiles - 1), tiles)
             for b in range(blocks):
                 done = (before, blocks - 1) if b == 0 else (i, b - 1)
-                soon = (i, b + 1) if b < blocks - 1 else (tile_of(j + 1), 0)
                 beside = {}
                 for part in range(2):
-                    beside[8 * part + 3] = functools.partial(relate, n, *soon, part)
                     for kind in range(2):
                         beside[8 * part + 4 * kind + 1] = functools.partial(gain, n, *done, kind, part)
-                weigh(b, beside)
+                weigh(n, i, b, beside)
             if final:
 
                 @pl.when(j > 0)
@@ -436,7 +428,6 @@
             pltpu.VMEM((lines * stars, KDIM), BF16),
             pltpu.VMEM((KDIM, 2 * group * slots), BF16),
             pltpu.VMEM((SOURCES, lines * stars), BF16),
-            pltpu.VMEM((blocks, TILE, 2 * TILE), F32),
             pltpu.VMEM((blocks, 2, 2 * TILE, TILE), BF16),
             pltpu.VMEM((tiles + 1, 2, SOURCES, TILE), F32),
             pltpu.SemaphoreType.DMA((7,)),

time: 42.8 us -> 43.3 us (1.012)
  Pallas kernels: 40.8 us -> 41.3 us
    pallas_call x1, Pallas kernels: 39.5 us -> 39.9 us  [body(): pl.pallas_call(functools.partial(kernel, lines, planes), out_shape=jax.Sh...]
where the time goes in v8:
time: 43.3 us; the launch traced here: 42.6 us
  Pallas kernels  41.3 us (95%)
  between operations  1.29 us (3%)
    pallas_call x1, Pallas kernels, body(): pl.pallas_call(functools.partial(kernel, lines, planes), out_shape=jax.Sh...  39.9 us
    pallas_call x1, Pallas kernels, body(): pl.pallas_call(correct_kernel, out_shape=(three,) * 4, in_specs=[pl.Block...  1.33 us

profile of v8, /device:TPU:224, one launch (start us, length us, event | category | flops | bytes accessed | tf_op | source)
XLA Modules:
  0.0 42.6 jit_solution(6327992547230357304)
XLA Ops:
  1.3 39.9 %forces.1.result = f32[24,64]{1,0:T(8,128)} custom-call(f32[3,384]{1,0:T(4,128)} %pos_hbm.1, f32[3,384]{1,0:T(4,128)} %vel_hbm.1, f32[3,384]{1,0:T(4,128)} %acc_hbm.1, f32[3,384]{1,0:T(4,128)} %jerk_hbm.1, f32[384]{0:T(512)} %mass_hbm.1, s32[384]{0:T(512)} %level_hbm.1, s32[1,64]{1,0:T(1,128)} %index_hbm.1), custom_call_target="tpu_custom_call" | custom-call | tf_op jit(solution)/shard_map/forces/pallas_call | solution.py:410
  41.2 1.3 %correct.1 = (f32[3,64]{1,0:T(4,128)}, f32[3,64]{1,0:T(4,128)}, f32[3,64]{1,0:T(4,128)}, f32[3,64]{1,0:T(4,128)}) custom-call(f32[24,64]{1,0:T(8,128)} %forces.1.result, s32[1]{0:T(128)S(6)} %copy.12.count), custom_call_target="tpu_custom_call" | custom-call | tf_op jit(solution)/shard_map/correct/pallas_call | solution.py:446

commit v9 on v8

--- a/solution.py
+++ b/solution.py
@@ -117,7 +117,7 @@
 def kernel(
     lines, planes, pos_hbm, vel_hbm, acc_hbm, jerk_hbm, mass_hbm, level_hbm, index_hbm, result,
     pos, vel, acc, jerk, mass, level, index, stage, fields, actives, arrived, partial,
-    left, along, moments, high_low, sums,
+    left, along, moments, both, high_low, sums,
     load_sem, ready, field_send, field_recv, active_send, active_recv, part_send, part_recv,
 ):
     group = 2 * planes
@@ -268,14 +268,18 @@
     def stars_of(n, b):
         return pl.ds(pl.multiple_of((n * blocks + b) * TILE, TILE), TILE)
 
-    def weigh(n, i, b, beside):
+    def relate(n, i, side):
+        rows = pl.ds(pl.multiple_of(n * blocks * TILE, TILE), blocks * TILE)
         cols = pl.ds(pl.multiple_of(i * 2 * TILE, 2 * TILE), 2 * TILE)
-        both = jnp.dot(left[stars_of(n, b), :], along[:, cols], preferred_element_type=F32)
+        both[side] = jnp.dot(left[rows, :], along[:, cols], preferred_element_type=F32)
+
+    def weigh(b, side, beside):
         for sub in range(0, TILE, ROWS):
-            inverse = lax.rsqrt(both[sub:sub + ROWS, 0:TILE])
+            at = slice(b * TILE + sub, b * TILE + sub + ROWS)
+            inverse = lax.rsqrt(both[side, at, 0:TILE])
             inverse2 = inverse * inverse
             w = inverse2 * inverse
-            sw = (w * inverse2) * both[sub:sub + ROWS, TILE:2 * TILE]
+            sw = (w * inverse2) * both[side, at, TILE:2 * TILE]
             for kind, value in enumerate((w, sw)):
                 high = value.astype(BF16)
                 high_low[b, kind, sub:sub + ROWS, :] = high
@@ -309,32 +313,36 @@
     sums[...] = jnp.zeros_like(sums)
 
     def pair_round(n, final):
-
-        def slot_tile(j, carry):
-            i = tile_of(j)
-            before = jnp.where(j > 0, tile_of(j + tiles - 1), tiles)
-            for b in range(blocks):
-                done = (before, blocks - 1) if b == 0 else (i, b - 1)
-                beside = {}
-                for part in range(2):
+        relate(n, tile_of(0), 0)
+
+        def two_tiles(pair, carry):
+            for side in range(2):
+                j = 2 * pair + side
+                i = tile_of(j)
+                before = tile_of(j + tiles - 1) if side else jnp.where(j > 0, tile_of(j + tiles - 1), tiles)
+                relate(n, tile_of(j + 1), 1 - side)
+                for b in range(blocks):
+                    done = (before, blocks - 1) if b == 0 else (i, b - 1)
+                    beside = {}
                     for kind in range(2):
-                        beside[8 * part + 4 * kind + 1] = functools.partial(gain, n, *done, kind, part)
-                weigh(n, i, b, beside)
-            if final:
-
-                @pl.when(j > 0)
-                def _():
-                    finish(before)
-
-            else:
-
-                @pl.when((n == 0) & (j == 1) & (z // 2 % 2 == 0))
+                        for part in range(2):
+                            beside[4 * (2 * kind + part) + 1] = functools.partial(gain, n, *done, kind, part)
+                    weigh(b, side, beside)
+                if final:
+
+                    @pl.when(j > 0)
+                    def _():
+                        finish(before)
+
+            if not final:
+
+                @pl.when((n == 0) & (pair == 0) & (z // 2 % 2 == 0))
                 def _():
                     lax.fori_loop(z // 4 * 4 + 2, z // 4 * 4 + 4, send_higher, 0)
 
             return carry
 
-        lax.fori_loop(0, tiles, slot_tile, 0, unroll=1 if final else 2)
+        lax.fori_loop(0, tiles // 2, two_tiles, 0)
         for kind in range(2):
             for part in range(2):
                 gain(n, tile_of(tiles - 1), blocks - 1, kind, part)
@@ -428,6 +436,7 @@
             pltpu.VMEM((lines * stars, KDIM), BF16),
             pltpu.VMEM((KDIM, 2 * group * slots), BF16),
             pltpu.VMEM((SOURCES, lines * stars), BF16),
+            pltpu.VMEM((2, 2 * stars, 2 * TILE), F32),
             pltpu.VMEM((blocks, 2, 2 * TILE, TILE), BF16),
             pltpu.VMEM((tiles + 1, 2, SOURCES, TILE), F32),
             pltpu.SemaphoreType.DMA((7,)),

time: 43.3 us -> 45.4 us (1.048)
  Pallas kernels: 41.3 us -> 43.4 us
    pallas_call x1, Pallas kernels: 39.9 us -> 42 us  [body(): pl.pallas_call(functools.partial(kernel, lines, planes), out_shape=jax.Sh...]
where the time goes in v9:
time: 45.4 us; the launch traced here: 44.7 us
  Pallas kernels  43.4 us (96%)
  between operations  1.29 us (3%)
    pallas_call x1, Pallas kernels, body(): pl.pallas_call(functools.partial(kernel, lines, planes), out_shape=jax.Sh...  42 us
    pallas_call x1, Pallas kernels, body(): pl.pallas_call(correct_kernel, out_shape=(three,) * 4, in_specs=[pl.Block...  1.33 us

profile of v9, /device:TPU:224, one launch (start us, length us, event | category | flops | bytes accessed | tf_op | source)
XLA Modules:
  0.0 44.7 jit_solution(12467489164155754282)
XLA Ops:
  1.3 42.0 %forces.1.result = f32[24,64]{1,0:T(8,128)} custom-call(f32[3,384]{1,0:T(4,128)} %pos_hbm.1, f32[3,384]{1,0:T(4,128)} %vel_hbm.1, f32[3,384]{1,0:T(4,128)} %acc_hbm.1, f32[3,384]{1,0:T(4,128)} %jerk_hbm.1, f32[384]{0:T(512)} %mass_hbm.1, s32[384]{0:T(512)} %level_hbm.1, s32[1,64]{1,0:T(1,128)} %index_hbm.1), custom_call_target="tpu_custom_call" | custom-call | tf_op jit(solution)/shard_map/forces/pallas_call | solution.py:418
  43.3 1.3 %correct.1 = (f32[3,64]{1,0:T(4,128)}, f32[3,64]{1,0:T(4,128)}, f32[3,64]{1,0:T(4,128)}, f32[3,64]{1,0:T(4,128)}) custom-call(f32[24,64]{1,0:T(8,128)} %forces.1.result, s32[1]{0:T(128)S(6)} %copy.12.count), custom_call_target="tpu_custom_call" | custom-call | tf_op jit(solution)/shard_map/correct/pallas_call | solution.py:455

commit v10 on v7

--- a/solution.py
+++ b/solution.py
@@ -14,8 +14,10 @@
 BF16 = jnp.bfloat16
 LANES = 128
 TILE = 256
+QUARTER = 64
 KDIM = 128
 ROWS = 16
+UNROLL = 1
 SOURCES = 32
 VMEM_LIMIT = 63 * 1024 * 1024
 
@@ -269,10 +271,12 @@
         return pl.ds(pl.multiple_of((n * blocks + b) * TILE, TILE), TILE)
 
     def relate(n, i, b, part):
-        half = slice(part * TILE // 2, (part + 1) * TILE // 2)
-        rows = pl.ds(pl.multiple_of((n * blocks + b) * TILE + part * TILE // 2, TILE // 2), TILE // 2)
+        rows = pl.ds(pl.multiple_of((n * blocks + b) * TILE + part * QUARTER, QUARTER), QUARTER)
         cols = pl.ds(pl.multiple_of(i * 2 * TILE, 2 * TILE), 2 * TILE)
-        both[b, half, :] = jnp.dot(left[rows, :], along[:, cols], preferred_element_type=F32)
+        return jnp.dot(left[rows, :], along[:, cols], preferred_element_type=F32)
+
+    def keep(b, part, value):
+        both[b, part * QUARTER:(part + 1) * QUARTER, :] = value
 
     def weigh(b, beside):
         for sub in range(0, TILE, ROWS):
@@ -284,12 +288,11 @@
                 high = value.astype(BF16)
                 high_low[b, kind, sub:sub + ROWS, :] = high
                 high_low[b, kind, TILE + sub:TILE + sub + ROWS, :] = (value - high.astype(F32)).astype(BF16)
-            if sub // ROWS in beside:
-                beside[sub // ROWS]()
-
-    def gain(n, i, b, kind, part):
+            beside(sub // ROWS)
+
+    def gain(n, b, kind, part):
         piece = high_low[b, kind, part * TILE:(part + 1) * TILE, :]
-        sums[i, kind] += jnp.dot(moments[:, stars_of(n, b)], piece, preferred_element_type=F32)
+        return jnp.dot(moments[:, stars_of(n, b)], piece, preferred_element_type=F32)
 
     def finish(i):
         by_w, by_s = sums[i, 0], sums[i, 1]
@@ -312,58 +315,64 @@
 
     sums[...] = jnp.zeros_like(sums)
 
-    def pair_round(n, final):
-        for part in range(2):
-            relate(n, tile_of(0), 0, part)
-
-        def slot_tile(j, carry):
-            i = tile_of(j)
-            before = jnp.where(j > 0, tile_of(j + tiles - 1), tiles)
-            for b in range(blocks):
-                done = (before, blocks - 1) if b == 0 else (i, b - 1)
-                soon = (i, b + 1) if b < blocks - 1 else (tile_of(j + 1), 0)
-                beside = {}
-                for part in range(2):
-                    beside[8 * part + 3] = functools.partial(relate, n, *soon, part)
-                    for kind in range(2):
-                        beside[8 * part + 4 * kind + 1] = functools.partial(gain, n, *done, kind, part)
-                weigh(b, beside)
-            if final:
-
-                @pl.when(j > 0)
-                def _():
-                    finish(before)
-
-            else:
-
-                @pl.when((n == 0) & (j == 1) & (z // 2 % 2 == 0))
-                def _():
-                    lax.fori_loop(z // 4 * 4 + 2, z // 4 * 4 + 4, send_higher, 0)
-
-            return carry
-
-        lax.fori_loop(0, tiles, slot_tile, 0, unroll=1 if final else 2)
-        for kind in range(2):
-            for part in range(2):
-                gain(n, tile_of(tiles - 1), blocks - 1, kind, part)
-        if final:
-            finish(tile_of(tiles - 1))
-
-    def early_round(n, carry):
-        pair_round(n, False)
-
-        @pl.when(n == 0)
+    steps = TILE // ROWS
+    pieces_of = TILE // QUARTER
+
+    def locate(k):
+        return k // tiles, tile_of(k % tiles)
+
+    for part in range(pieces_of):
+        keep(0, part, relate(0, tile_of(0), 0, part))
+
+    def slot_tile(k, carry):
+        n, i = locate(k)
+        j = k % tiles
+        last_n, last_i = locate(jnp.where(k > 0, k - 1, 0))
+        last_i = jnp.where(k > 0, last_i, tiles)
+        next_n, next_i = locate(jnp.where(k < rounds * tiles - 1, k + 1, k))
+        for b in range(blocks):
+            done_n, done_i, done_b = (last_n, last_i, blocks - 1) if b == 0 else (n, i, b - 1)
+            soon_n, soon_i, soon_b = (n, i, b + 1) if b < blocks - 1 else (next_n, next_i, 0)
+            related, gained = {}, {}
+
+            def beside(step):
+                part, phase = step // (steps // pieces_of), step % (steps // pieces_of)
+                if phase == 0:
+                    related[part] = relate(soon_n, soon_i, soon_b, part)
+                if phase == 1:
+                    gained[part] = gain(done_n, done_b, part // 2, part % 2)
+                if phase == 2:
+                    keep(soon_b, part, related[part])
+                if phase == 3:
+                    sums[done_i, part // 2] += gained[part]
+
+            weigh(b, beside)
+
+        @pl.when((n == rounds - 1) & (j > 0))
         def _():
-            lax.fori_loop(z // 4 * 4 + 4, lines, send_higher, 0)
-
-        for k in (2 * n + 2, 2 * n + 3):
-            block = line_peer(k)
-            line_copy(block, block).wait_recv()
-            take_stars(k, block)
-        return carry
-
-    lax.fori_loop(0, rounds - 1, early_round, 0)
-    pair_round(rounds - 1, True)
+            finish(last_i)
+
+        @pl.when((n == 0) & (j == 1) & (z // 2 % 2 == 0) & (rounds > 1))
+        def _():
+            lax.fori_loop(z // 4 * 4 + 2, z // 4 * 4 + 4, send_higher, 0)
+
+        @pl.when((n < rounds - 1) & (j == tiles - 2))
+        def _():
+            @pl.when(n == 0)
+            def _():
+                lax.fori_loop(z // 4 * 4 + 4, lines, send_higher, 0)
+
+            for later in (2 * n + 2, 2 * n + 3):
+                block = line_peer(later)
+                line_copy(block, block).wait_recv()
+                take_stars(later, block)
+
+        return carry
+
+    lax.fori_loop(0, rounds * tiles, slot_tile, 0, unroll=UNROLL)
+    for part in range(4):
+        sums[tile_of(tiles - 1), part // 2] += gain(rounds - 1, blocks - 1, part // 2, part % 2)
+    finish(tile_of(tiles - 1))
 
     arrived[me] = partial[me // 2]
 

time: 42.8 us -> 44.8 us (1.047)
  Pallas kernels: 40.8 us -> 43.1 us
    pallas_call x1, Pallas kernels: 39.5 us -> 41.7 us  [body(): pl.pallas_call(functools.partial(kernel, lines, planes), out_shape=jax.Sh...]
where the time goes in v10:
time: 44.8 us; the launch traced here: 44.4 us
  Pallas kernels  43.1 us (96%)
  between operations  1.29 us (3%)
    pallas_call x1, Pallas kernels, body(): pl.pallas_call(functools.partial(kernel, lines, planes), out_shape=jax.Sh...  41.7 us
    pallas_call x1, Pallas kernels, body(): pl.pallas_call(correct_kernel, out_shape=(three,) * 4, in_specs=[pl.Block...  1.33 us

profile of v10, /device:TPU:224, one launch (start us, length us, event | category | flops | bytes accessed | tf_op | source)
XLA Modules:
  0.0 44.4 jit_solution(1840022923148247102)
XLA Ops:
  1.3 41.7 %forces.1.result = f32[24,64]{1,0:T(8,128)} custom-call(f32[3,384]{1,0:T(4,128)} %pos_hbm.1, f32[3,384]{1,0:T(4,128)} %vel_hbm.1, f32[3,384]{1,0:T(4,128)} %acc_hbm.1, f32[3,384]{1,0:T(4,128)} %jerk_hbm.1, f32[384]{0:T(512)} %mass_hbm.1, s32[384]{0:T(512)} %level_hbm.1, s32[1,64]{1,0:T(1,128)} %index_hbm.1), custom_call_target="tpu_custom_call" | custom-call | tf_op jit(solution)/shard_map/forces/pallas_call | solution.py:427
  43.0 1.3 %correct.1 = (f32[3,64]{1,0:T(4,128)}, f32[3,64]{1,0:T(4,128)}, f32[3,64]{1,0:T(4,128)}, f32[3,64]{1,0:T(4,128)}) custom-call(f32[24,64]{1,0:T(8,128)} %forces.1.result, s32[1]{0:T(128)S(6)} %copy.12.count), custom_call_target="tpu_custom_call" | custom-call | tf_op jit(solution)/shard_map/correct/pallas_call | solution.py:464

commit v11 on v10

--- a/solution.py
+++ b/solution.py
@@ -14,10 +14,9 @@
 BF16 = jnp.bfloat16
 LANES = 128
 TILE = 256
-QUARTER = 64
+PART = 128
 KDIM = 128
 ROWS = 16
-UNROLL = 1
 SOURCES = 32
 VMEM_LIMIT = 63 * 1024 * 1024
 
@@ -271,12 +270,12 @@
         return pl.ds(pl.multiple_of((n * blocks + b) * TILE, TILE), TILE)
 
     def relate(n, i, b, part):
-        rows = pl.ds(pl.multiple_of((n * blocks + b) * TILE + part * QUARTER, QUARTER), QUARTER)
+        rows = pl.ds(pl.multiple_of((n * blocks + b) * TILE + part * PART, PART), PART)
         cols = pl.ds(pl.multiple_of(i * 2 * TILE, 2 * TILE), 2 * TILE)
         return jnp.dot(left[rows, :], along[:, cols], preferred_element_type=F32)
 
     def keep(b, part, value):
-        both[b, part * QUARTER:(part + 1) * QUARTER, :] = value
+        both[b, part * PART:(part + 1) * PART, :] = value
 
     def weigh(b, beside):
         for sub in range(0, TILE, ROWS):
@@ -316,7 +315,7 @@
     sums[...] = jnp.zeros_like(sums)
 
     steps = TILE // ROWS
-    pieces_of = TILE // QUARTER
+    pieces_of = TILE // PART
 
     def locate(k):
         return k // tiles, tile_of(k % tiles)
@@ -324,39 +323,40 @@
     for part in range(pieces_of):
         keep(0, part, relate(0, tile_of(0), 0, part))
 
-    def slot_tile(k, carry):
-        n, i = locate(k)
-        j = k % tiles
-        last_n, last_i = locate(jnp.where(k > 0, k - 1, 0))
-        last_i = jnp.where(k > 0, last_i, tiles)
-        next_n, next_i = locate(jnp.where(k < rounds * tiles - 1, k + 1, k))
-        for b in range(blocks):
-            done_n, done_i, done_b = (last_n, last_i, blocks - 1) if b == 0 else (n, i, b - 1)
-            soon_n, soon_i, soon_b = (n, i, b + 1) if b < blocks - 1 else (next_n, next_i, 0)
-            related, gained = {}, {}
-
-            def beside(step):
-                part, phase = step // (steps // pieces_of), step % (steps // pieces_of)
-                if phase == 0:
-                    related[part] = relate(soon_n, soon_i, soon_b, part)
-                if phase == 1:
-                    gained[part] = gain(done_n, done_b, part // 2, part % 2)
-                if phase == 2:
-                    keep(soon_b, part, related[part])
-                if phase == 3:
-                    sums[done_i, part // 2] += gained[part]
-
-            weigh(b, beside)
-
-        @pl.when((n == rounds - 1) & (j > 0))
+    def two_tiles(pair, carry):
+        for k in (2 * pair, 2 * pair + 1):
+            n, i = locate(k)
+            last_n, last_i = locate(jnp.where(k > 0, k - 1, 0))
+            last_i = jnp.where(k > 0, last_i, tiles)
+            next_n, next_i = locate(jnp.where(k < rounds * tiles - 1, k + 1, k))
+            for b in range(blocks):
+                done_n, done_i, done_b = (last_n, last_i, blocks - 1) if b == 0 else (n, i, b - 1)
+                soon_n, soon_i, soon_b = (n, i, b + 1) if b < blocks - 1 else (next_n, next_i, 0)
+
+                def beside(step):
+                    part, phase = step // (steps // 4), step % (steps // 4)
+                    if phase == 1:
+                        sums[done_i, part // 2] += gain(done_n, done_b, part // 2, part % 2)
+                    if phase == 3 and part % (4 // pieces_of) == 0:
+                        keep(soon_b, part * pieces_of // 4, relate(soon_n, soon_i, soon_b, part * pieces_of // 4))
+
+                weigh(b, beside)
+
+        n, j = 2 * pair // tiles, 2 * pair % tiles
+
+        @pl.when(n == rounds - 1)
         def _():
-            finish(last_i)
-
-        @pl.when((n == 0) & (j == 1) & (z // 2 % 2 == 0) & (rounds > 1))
+            @pl.when(j > 0)
+            def _():
+                finish(tile_of(j + tiles - 1))
+
+            finish(tile_of(j))
+
+        @pl.when((n == 0) & (j == 0) & (z // 2 % 2 == 0) & (rounds > 1))
         def _():
             lax.fori_loop(z // 4 * 4 + 2, z // 4 * 4 + 4, send_higher, 0)
 
-        @pl.when((n < rounds - 1) & (j == tiles - 2))
+        @pl.when((n < rounds - 1) & (j == tiles - 4))
         def _():
             @pl.when(n == 0)
             def _():
@@ -369,7 +369,7 @@
 
         return carry
 
-    lax.fori_loop(0, rounds * tiles, slot_tile, 0, unroll=UNROLL)
+    lax.fori_loop(0, rounds * tiles // 2, two_tiles, 0)
     for part in range(4):
         sums[tile_of(tiles - 1), part // 2] += gain(rounds - 1, blocks - 1, part // 2, part % 2)
     finish(tile_of(tiles - 1))

time: 44.8 us -> 40.8 us (0.911)
  Pallas kernels: 43.1 us -> 39.3 us
    pallas_call x1, Pallas kernels: 41.7 us -> 38 us  [body(): pl.pallas_call(functools.partial(kernel, lines, planes), out_shape=jax.Sh...]
where the time goes in v11:
time: 40.8 us; the launch traced here: 40.6 us
  Pallas kernels  39.3 us (96%)
  between operations  1.29 us (3%)
    pallas_call x1, Pallas kernels, body(): pl.pallas_call(functools.partial(kernel, lines, planes), out_shape=jax.Sh...  38 us
    pallas_call x1, Pallas kernels, body(): pl.pallas_call(correct_kernel, out_shape=(three,) * 4, in_specs=[pl.Block...  1.33 us

profile of v11, /device:TPU:224, one launch (start us, length us, event | category | flops | bytes accessed | tf_op | source)
XLA Modules:
  0.0 40.6 jit_solution(15065862347531464185)
XLA Ops:
  1.3 38.0 %forces.1.result = f32[24,64]{1,0:T(8,128)} custom-call(f32[3,384]{1,0:T(4,128)} %pos_hbm.1, f32[3,384]{1,0:T(4,128)} %vel_hbm.1, f32[3,384]{1,0:T(4,128)} %acc_hbm.1, f32[3,384]{1,0:T(4,128)} %jerk_hbm.1, f32[384]{0:T(512)} %mass_hbm.1, s32[384]{0:T(512)} %level_hbm.1, s32[1,64]{1,0:T(1,128)} %index_hbm.1), custom_call_target="tpu_custom_call" | custom-call | tf_op jit(solution)/shard_map/forces/pallas_call | solution.py:427
  39.3 1.3 %correct.1 = (f32[3,64]{1,0:T(4,128)}, f32[3,64]{1,0:T(4,128)}, f32[3,64]{1,0:T(4,128)}, f32[3,64]{1,0:T(4,128)}) custom-call(f32[24,64]{1,0:T(8,128)} %forces.1.result, s32[1]{0:T(128)S(6)} %copy.12.count), custom_call_target="tpu_custom_call" | custom-call | tf_op jit(solution)/shard_map/correct/pallas_call | solution.py:464

commit v12 on v11

--- a/solution.py
+++ b/solution.py
@@ -14,7 +14,7 @@
 BF16 = jnp.bfloat16
 LANES = 128
 TILE = 256
-PART = 128
+PART = 256
 KDIM = 128
 ROWS = 16
 SOURCES = 32

time: 40.8 us -> 40.9 us (level)
  no operation moved by 1% of the time
where the time goes in v12:
time: 40.9 us; the launch traced here: 40.7 us
  Pallas kernels  39.4 us (96%)
  between operations  1.29 us (3%)
    pallas_call x1, Pallas kernels, body(): pl.pallas_call(functools.partial(kernel, lines, planes), out_shape=jax.Sh...  38.1 us
    pallas_call x1, Pallas kernels, body(): pl.pallas_call(correct_kernel, out_shape=(three,) * 4, in_specs=[pl.Block...  1.33 us

profile of v12, /device:TPU:224, one launch (start us, length us, event | category | flops | bytes accessed | tf_op | source)
XLA Modules:
  0.0 40.7 jit_solution(12086684691545563285)
XLA Ops:
  1.3 38.1 %forces.1.result = f32[24,64]{1,0:T(8,128)} custom-call(f32[3,384]{1,0:T(4,128)} %pos_hbm.1, f32[3,384]{1,0:T(4,128)} %vel_hbm.1, f32[3,384]{1,0:T(4,128)} %acc_hbm.1, f32[3,384]{1,0:T(4,128)} %jerk_hbm.1, f32[384]{0:T(512)} %mass_hbm.1, s32[384]{0:T(512)} %level_hbm.1, s32[1,64]{1,0:T(1,128)} %index_hbm.1), custom_call_target="tpu_custom_call" | custom-call | tf_op jit(solution)/shard_map/forces/pallas_call | solution.py:427
  39.4 1.3 %correct.1 = (f32[3,64]{1,0:T(4,128)}, f32[3,64]{1,0:T(4,128)}, f32[3,64]{1,0:T(4,128)}, f32[3,64]{1,0:T(4,128)}) custom-call(f32[24,64]{1,0:T(8,128)} %forces.1.result, s32[1]{0:T(128)S(6)} %copy.12.count), custom_call_target="tpu_custom_call" | custom-call | tf_op jit(solution)/shard_map/correct/pallas_call | solution.py:464

commit v13 on v12

--- a/solution.py
+++ b/solution.py
@@ -16,7 +16,7 @@
 TILE = 256
 PART = 256
 KDIM = 128
-ROWS = 16
+ROWS = 32
 SOURCES = 32
 VMEM_LIMIT = 63 * 1024 * 1024
 
@@ -337,7 +337,7 @@
                     part, phase = step // (steps // 4), step % (steps // 4)
                     if phase == 1:
                         sums[done_i, part // 2] += gain(done_n, done_b, part // 2, part % 2)
-                    if phase == 3 and part % (4 // pieces_of) == 0:
+                    if phase == steps // 4 - 1 and part % (4 // pieces_of) == 0:
                         keep(soon_b, part * pieces_of // 4, relate(soon_n, soon_i, soon_b, part * pieces_of // 4))
 
                 weigh(b, beside)

time: 40.9 us -> 40.9 us (level)
  no operation moved by 1% of the time
where the time goes in v13:
time: 40.9 us; the launch traced here: 40.7 us
  Pallas kernels  39.4 us (96%)
  between operations  1.29 us (3%)
    pallas_call x1, Pallas kernels, body(): pl.pallas_call(functools.partial(kernel, lines, planes), out_shape=jax.Sh...  38.1 us
    pallas_call x1, Pallas kernels, body(): pl.pallas_call(correct_kernel, out_shape=(three,) * 4, in_specs=[pl.Block...  1.33 us

profile of v13, /device:TPU:224, one launch (start us, length us, event | category | flops | bytes accessed | tf_op | source)
XLA Modules:
  0.0 40.7 jit_solution(12086684691545563285)
XLA Ops:
  1.3 38.1 %forces.1.result = f32[24,64]{1,0:T(8,128)} custom-call(f32[3,384]{1,0:T(4,128)} %pos_hbm.1, f32[3,384]{1,0:T(4,128)} %vel_hbm.1, f32[3,384]{1,0:T(4,128)} %acc_hbm.1, f32[3,384]{1,0:T(4,128)} %jerk_hbm.1, f32[384]{0:T(512)} %mass_hbm.1, s32[384]{0:T(512)} %level_hbm.1, s32[1,64]{1,0:T(1,128)} %index_hbm.1), custom_call_target="tpu_custom_call" | custom-call | tf_op jit(solution)/shard_map/forces/pallas_call | solution.py:427
  39.4 1.3 %correct.1 = (f32[3,64]{1,0:T(4,128)}, f32[3,64]{1,0:T(4,128)}, f32[3,64]{1,0:T(4,128)}, f32[3,64]{1,0:T(4,128)}) custom-call(f32[24,64]{1,0:T(8,128)} %forces.1.result, s32[1]{0:T(128)S(6)} %copy.12.count), custom_call_target="tpu_custom_call" | custom-call | tf_op jit(solution)/shard_map/correct/pallas_call | solution.py:464
